TPU v7x, 256 devices: a whole 4x4x8 slice. The times are simulated.
256 devices in a mesh: dp: 2 (over x_hi), tm: 16 (over x_lo, z), space: 8 (over y, core).
Axes of the slice: x: 4 (x_hi: 2, x_lo: 2; x = x_hi * 2 + x_lo), y: 4, z: 8, core: 2. Of those that a mesh axis runs over, the one named last changes fastest.
Arguments:
- tokens: bfloat16 [2, 16, 1024, 1152], P('dp', 'tm', 'space'), may hold values from -6 to 6
- validity: int32 [1024], replicated, may hold values from 0 to 1, as said below
- table_space: float32 [3, 1152], replicated, may hold values from -3 to 3
- qkv_space: bfloat16 [1152, 1728], replicated, may hold values from -0.6 to 0.6
- gains_space: float32 [2, 72], replicated, may hold values from 0.5 to 6
- out_space: bfloat16 [576, 1152], replicated, may hold values from -0.25 to 0.25
- table_time: float32 [3, 1152], replicated, may hold values from -3 to 3
- qkv_time: bfloat16 [1152, 1728], replicated, may hold values from -0.6 to 0.6
- gains_time: float32 [2, 72], replicated, may hold values from 0.5 to 6
- out_time: bfloat16 [576, 1152], replicated, may hold values from -0.25 to 0.25
- cotangent: bfloat16 [2, 16, 1024, 1152], P('dp', 'tm', 'space'), may hold values from -6 to 6
Outputs:
- mixed: bfloat16 [2, 16, 1024, 1152], P('dp', 'tm', 'space')
- token_grad: bfloat16 [2, 16, 1024, 1152], P('dp', 'tm', 'space')
- grad_out_space: float32 [576, 1152], P('space', ('dp', 'tm'))
- grad_out_time: float32 [576, 1152], P('space', ('dp', 'tm'))
- grad_tables: float32 [2, 3, 1152], replicated
Inputs may be any that keep to these rules, and one draw needn't show every extreme that they name: `validity`: exactly 1014 of the 1024 entries are 1.
All inputs are finite; a program needn't handle non-finite values.
Results may differ from a plain program's by a relative error of at most 0.03.
Values may be sent and summed in bfloat16 or wider, within the bound.
A program may use at most 128 MiB of HBM per device.

v0:
```python
import functools

import jax
import jax.numpy as jnp
from jax import lax
from jax.experimental import pallas as pl
from jax.experimental.pallas import tpu as pltpu
from jax.sharding import PartitionSpec as P

MESH = pl.DeviceIdType.MESH
BF = jnp.bfloat16
F32 = jnp.float32
EPSILON = 1e-6

NN = (((1,), (0,)), ((), ()))
NT = (((1,), (1,)), ((), ()))
TN = (((0,), (0,)), ((), ()))


def dot(a, b, dims=NN):
    return lax.dot_general(a, b, dims, preferred_element_type=F32)


def mean(v):
    return jnp.mean(v, axis=-1, keepdims=True)


def norm(values):
    centred = values - mean(values)
    inv_std = lax.rsqrt(mean(centred * centred) + EPSILON)
    return centred * inv_std, inv_std


def rms_scale(raw):
    return lax.rsqrt(mean(raw * raw) + EPSILON)


def rms_back(grad, raw):
    inv = rms_scale(raw)
    return inv * (grad - raw * (inv * inv) * mean(grad * raw))


def modulate_back(grad, normed, inv_std, table):
    grad_norm = grad * (1.0 + table[1:2, :])
    grad_in = inv_std * (grad_norm - mean(grad_norm) - normed * mean(grad_norm * normed))
    shift = jnp.sum(grad, axis=0, keepdims=True)
    scale = jnp.sum(grad * normed, axis=0, keepdims=True)
    return grad_in, shift, scale


class Sizes:
    pass


def to_blocks(rows, cut):
    n, width = rows.shape[0] // 8, rows.shape[1]
    cube = rows.reshape(n, 8, width)
    low = jnp.concatenate([cube[:, :, cut:], jnp.zeros((n, 8, 2 * cut - width), F32)], axis=2)
    return jnp.concatenate([cube[:, :, :cut], low], axis=1).astype(BF)


def from_blocks(blocks, width):
    n, _, cut = blocks.shape
    cube = blocks.astype(F32)
    full = jnp.concatenate([cube[:, :8, :], cube[:, 8:, : width - cut]], axis=2)
    return full.reshape(n * 8, width)


def to_lines(rows, lines):
    third = rows[0].shape[1] // 3
    parts = [r[:, third * c : third * (c + 1)] for r in rows for c in range(3)]
    if lines > len(parts):
        parts.append(jnp.zeros((lines - len(parts), third), F32))
    return jnp.concatenate(parts, axis=0)


def from_lines(lines, r):
    return jnp.concatenate([lines[3 * r + c : 3 * r + c + 1, :] for c in range(3)], axis=1)


def kernel(z, names, *refs):
    r = Sizes()
    for name, ref in zip(names, refs):
        setattr(r, name, ref)
    heads, hd, width, toks, ns, nt, nz, cut = (
        z.heads, z.hd, z.width, z.toks, z.ns, z.nt, z.nz, z.cut,
    )
    att_w = heads * hd
    scaling = hd ** (-0.5)
    dp = lax.axis_index("dp")
    tm = lax.axis_index("tm")
    sp = lax.axis_index("space")
    core, y = sp % 2, sp // 2
    x_lo, zz = tm // nz, tm % nz
    x = dp * 2 + x_lo
    nx = 4
    ny = ns // 2

    def remote(src, dst, send_sem, recv_sem, device):
        return pltpu.make_async_remote_copy(
            src_ref=src, dst_ref=dst, send_sem=send_sem, recv_sem=recv_sem,
            device_id=device, device_id_type=MESH,
        )

    groups = {
        "space": (ns, sp, lambda j: (dp, tm, j)),
        "tm": (nt, tm, lambda j: (dp, j, sp)),
        "y": (ny, y, lambda j: (dp, tm, j * 2 + core)),
        "x": (nx, x, lambda j: (j // 2, (j % 2) * nz + zz, sp)),
        "z": (nz, zz, lambda j: (dp, x_lo * nz + j, sp)),
    }

    def exchange(group, src_of, recv, sems, d):
        n, me, device = groups[group]
        j = (me + d) % n
        return remote(src_of(j), recv.at[me], sems.at[0, d], sems.at[1, me], device(j))

    def start_all(group, src_of, recv, sems):
        n = groups[group][0]

        def body(d, carry):
            exchange(group, src_of, recv, sems, d).start()
            return carry

        lax.fori_loop(1, n, body, 0)

    def wait_from(group, src_of, recv, sems, j):
        n, me, device = groups[group]
        remote(src_of(j), recv.at[j], sems.at[0, 0], sems.at[1, j], device(j)).wait_recv()

    def wait_all(group, src_of, recv, sems):
        n, me, _ = groups[group]

        def body(d, carry):
            wait_from(group, src_of, recv, sems, (me + d) % n)
            return carry

        lax.fori_loop(1, n, body, 0)

    def wait_sent(group, src_of, recv, sems):
        n = groups[group][0]

        def body(d, carry):
            exchange(group, src_of, recv, sems, d).wait_send()
            return carry

        lax.fori_loop(1, n, body, 0)

    weight_copies = [
        pltpu.make_async_copy(src, dst, r.w_sem.at[i])
        for i, (src, dst) in enumerate(
            [(r.qkv_s, r.wqs), (r.out_s, r.wos), (r.qkv_t, r.wqt), (r.out_t, r.wot)]
        )
    ]
    for copy in weight_copies:
        copy.start()
    barrier = pltpu.get_barrier_semaphore()

    def signal(device):
        pl.semaphore_signal(barrier, inc=1, device_id=device, device_id_type=MESH)

    def greet(group):
        n, me, device = groups[group]

        def body(d, carry):
            signal(device((me + d) % n))
            return carry

        lax.fori_loop(1, n, body, 0)

    greet("space")
    greet("tm")
    other = 1 - dp
    signal((other, tm, sp))
    signal((other, (1 - x_lo) * nz + zz, sp))

    val = r.val[...].astype(F32)
    key_row = jnp.concatenate([val[j : j + 1, :] for j in range(ns)], axis=1)
    own_row = r.val[pl.ds(sp, 1), :].astype(F32)
    row_id = lax.broadcasted_iota(jnp.int32, (toks, toks), 0)
    col_id = lax.broadcasted_iota(jnp.int32, (toks, toks), 1)
    own = jnp.broadcast_to(own_row, (toks, toks))
    mask_s = jnp.sum(jnp.where(row_id == col_id, own, 0.0), axis=1, keepdims=True)
    mask_t = jnp.sum(jnp.where(tm * 8 + row_id % 8 == col_id, own, 0.0), axis=1, keepdims=True)

    def project(shifted, weight, gains, raw_ref, emit):
        raw_ref[...] = dot(shifted, weight)
        g = gains[...]
        for h in range(heads):
            base = 3 * hd * h
            p0 = raw_ref[:, base : base + hd]
            p1 = raw_ref[:, base + hd : base + 2 * hd]
            p2 = raw_ref[:, base + 2 * hd : base + 3 * hd]
            emit(h, p0 * rms_scale(p0) * g[0:1, :], p1 * rms_scale(p1) * g[1:2, :], p2)

    def project_back(h, dq, dk, dv, raw_ref, gains):
        g = gains[...]
        base = 3 * hd * h
        p0 = raw_ref[:, base : base + hd]
        p1 = raw_ref[:, base + hd : base + 2 * hd]
        r.grw[:, base : base + hd] = rms_back(dq * g[0:1, :], p0)
        r.grw[:, base + hd : base + 2 * hd] = rms_back(dk * g[1:2, :], p1)
        r.grw[:, base + 2 * hd : base + 3 * hd] = dv

    tokens = r.tok[...].astype(F32)
    table_s = r.tab_s[...]
    normed, _ = norm(tokens)
    shifted = (normed * (1.0 + table_s[1:2, :]) + table_s[0:1, :]).astype(BF)
    r.cot_send[...] = to_blocks(r.cot[...].astype(F32), cut)
    r.cot_recv[tm] = r.cot_send[tm]

    weight_copies[0].wait()

    def emit_s(h, q, k, v):
        packed = jnp.concatenate([q, k, v, jnp.zeros((toks, 256 - 3 * hd), F32)], axis=1)
        r.ps_send[h] = packed.astype(BF)

    project(shifted, r.wqs[...], r.gn_s, r.raw_s, emit_s)
    r.ps_recv[sp] = r.ps_send[sp]

    pl.semaphore_wait(barrier, ns - 1 + nt - 1 + 2)
    ps = ("space", lambda j: r.ps_send.at[j], r.ps_recv, r.ps_sem)
    start_all(*ps)
    ct = ("tm", lambda j: r.cot_send.at[j], r.cot_recv, r.cot_sem)
    start_all(*ct)
    wait_all(*ps)

    for j in range(ns):
        block = r.ps_recv[j].astype(F32)
        r.q_ref[j] = block[:, :hd].astype(BF)
        r.k_ref[toks * j : toks * (j + 1), :] = block[:, hd : 2 * hd].astype(BF)
        r.v_ref[toks * j : toks * (j + 1), :] = block[:, 2 * hd : 3 * hd].astype(BF)

    at = ("space", lambda j: r.at_send.at[j], r.at_recv, r.at_sem)

    def attend(d, carry):
        j = (sp + d) % ns
        scores = dot(r.q_ref[j], r.k_ref[...], NT) * scaling
        scores = jnp.where(key_row > 0.5, scores, -1e30)
        exps = jnp.exp(scores - jnp.max(scores, axis=-1, keepdims=True))
        weights = exps * (1.0 / jnp.sum(exps, axis=-1, keepdims=True))
        r.prob[j] = weights
        r.at_send[j] = dot(weights.astype(BF), r.v_ref[...]).astype(BF)

        @pl.when(d < ns)
        def _():
            exchange(*at, d).start()

        return carry

    lax.fori_loop(1, ns + 1, attend, 0)
    r.at_recv[sp] = r.at_send[sp]
    wait_all(*at)
    for h in range(heads):
        r.att_f[:, hd * h : hd * (h + 1)] = r.at_recv[h].astype(F32)
    r.att_s[...] = r.att_f[...].astype(BF)
    weight_copies[1].wait()
    branch_s = dot(r.att_s[...], r.wos[...])
    r.branch_s[...] = branch_s
    middle = r.tok[...].astype(F32) + mask_s * table_s[2:3, :] * branch_s
    r.mid_send[...] = to_blocks(middle, cut)
    r.mid_recv[tm] = r.mid_send[tm]
    md = ("tm", lambda j: r.mid_send.at[j], r.mid_recv, r.mid_sem)
    start_all(*md)

    table_t = r.tab_t[...]
    wait_all(*ct)
    cot = from_blocks(r.cot_recv[...], width)
    masked = cot * mask_t
    grad_branch = (masked * table_t[2:3, :]).astype(BF)
    r.gb_t[...] = grad_branch
    weight_copies[3].wait()
    r.grad_att[...] = dot(grad_branch, r.wot[...], NT)

    wait_all(*md)
    middle = from_blocks(r.mid_recv[...], width)
    normed, inv_t = norm(middle)
    shifted = (normed * (1.0 + table_t[1:2, :]) + table_t[0:1, :]).astype(BF)
    weight_copies[2].wait()
    same = row_id % 8 == col_id % 8

    def emit_t(h, q, k, v):
        q, k, v = q.astype(BF), k.astype(BF), v.astype(BF)
        scores = jnp.where(same, dot(q, k, NT) * scaling, -1e30)
        exps = jnp.exp(scores - jnp.max(scores, axis=-1, keepdims=True))
        weights = exps * (1.0 / jnp.sum(exps, axis=-1, keepdims=True))
        rounded = weights.astype(BF)
        r.att_f[:, hd * h : hd * (h + 1)] = dot(rounded, v)
        grad_out = r.grad_att[:, hd * h : hd * (h + 1)].astype(BF)
        dv = dot(rounded, grad_out, TN)
        dw = dot(grad_out, v, NT)
        ds = weights * (dw - jnp.sum(dw * weights, axis=-1, keepdims=True)) * scaling
        ds = ds.astype(BF)
        dq = dot(ds, k)
        dk = dot(ds, q, TN)
        project_back(
            h,
            dq.astype(BF).astype(F32),
            dk.astype(BF).astype(F32),
            dv.astype(BF).astype(F32),
            r.raw_t,
            r.gn_t,
        )

    project(shifted, r.wqt[...], r.gn_t, r.raw_t, emit_t)
    grad_shifted = dot(r.grw[...].astype(BF), r.wqt[...], NT)
    normed, inv_t = norm(from_blocks(r.mid_recv[...], width))
    grad_in, shift_t, scale_t = modulate_back(grad_shifted, normed, inv_t, table_t)
    cot = from_blocks(r.cot_recv[...], width)
    r.gm_send[...] = to_blocks(cot + grad_in, cut)
    r.gm_recv[tm] = r.gm_send[tm]
    gm = ("tm", lambda j: r.gm_send.at[j], r.gm_recv, r.gm_sem)
    start_all(*gm)

    att_t = r.att_f[...].astype(BF)
    branch_t = dot(att_t, r.wot[...])
    middle = from_blocks(r.mid_recv[...], width)
    r.mix_send[...] = to_blocks(middle + mask_t * table_t[2:3, :] * branch_t, cut)
    r.mix_recv[tm] = r.mix_send[tm]
    mx = ("tm", lambda j: r.mix_send.at[j], r.mix_recv, r.mix_sem)
    start_all(*mx)
    gate_t = jnp.sum(from_blocks(r.cot_recv[...], width) * mask_t * branch_t, axis=0, keepdims=True)

    pair = (dp, tm, sp + 1 - 2 * core)

    def pair_copy(a):
        return remote(
            r.part.at[a, 1 - core], r.pair_recv.at[a], r.pair_sem.at[0, a], r.pair_sem.at[1, a], pair
        )

    def partial_grad(a, att, grad_branch):
        full = dot(att, grad_branch, TN)
        pad = jnp.zeros((z.rows - hd, width), F32)
        for h in range(heads):
            block = jnp.concatenate([full[hd * h : hd * (h + 1), :], pad], axis=0)
            r.part[a, h % 2, h // 2] = block.astype(BF)
        pair_copy(a).start()

    def rs_args(kind, a):
        send, recv, sems = {
            "y": (r.y_send, r.y_recv, r.y_sem),
            "x": (r.x_send, r.x_recv, r.x_sem),
            "z": (r.z_send, r.z_recv, r.z_sem),
        }[kind]
        return (kind, lambda j: send.at[a, j], recv.at[a], sems.at[a])

    def rs_y(a):
        pair_copy(a).wait_recv()
        r.y_send[a] = (r.part[a, core].astype(F32) + r.pair_recv[a].astype(F32)).astype(BF)
        r.y_recv[a, y] = r.y_send[a, y]
        start_all(*rs_args("y", a))

    def total(ref, a, n):
        value = ref[a, 0].astype(F32)
        for j in range(1, n):
            value = value + ref[a, j].astype(F32)
        return value

    def rs_x(a):
        wait_all(*rs_args("y", a))
        value = total(r.y_recv, a, ny)
        part_w = width // nx
        for j in range(nx):
            r.x_send[a, j] = value[:, part_w * j : part_w * (j + 1)].astype(BF)
        r.x_recv[a, x] = r.x_send[a, x]
        start_all(*rs_args("x", a))

    def rs_z(a):
        wait_all(*rs_args("x", a))
        value = total(r.x_recv, a, nx)
        part_w = width // nx // nz
        for j in range(nz):
            r.z_send[a, j] = value[:, part_w * j : part_w * (j + 1)].astype(BF)
        r.z_recv[a, zz] = r.z_send[a, zz]
        start_all(*rs_args("z", a))

    def rs_end(a, out_ref):
        wait_all(*rs_args("z", a))
        out_ref[...] = total(r.z_recv, a, nz)[:hd, :]

    partial_grad(0, att_t, r.gb_t[...])
    rs_y(0)

    wait_all(*gm)
    grad_mid = from_blocks(r.gm_recv[...], width)
    r.grad_mid[...] = grad_mid
    masked = grad_mid * mask_s
    grad_branch = (masked * table_s[2:3, :]).astype(BF)
    r.gb_s[...] = grad_branch
    grad_att = dot(grad_branch, r.wos[...], NT)
    for h in range(heads):
        r.do_send[h] = grad_att[:, hd * h : hd * (h + 1)].astype(BF)
    r.do_recv[sp] = r.do_send[sp]
    do = ("space", lambda j: r.do_send.at[j], r.do_recv, r.do_sem)
    start_all(*do)
    gate_s = jnp.sum(r.grad_mid[...] * mask_s * r.branch_s[...], axis=0, keepdims=True)
    partial_grad(1, r.att_s[...], r.gb_s[...])

    def table_args(kind, k):
        send, recv, sems = getattr(r, k + kind + "_send"), getattr(r, k + kind + "_recv"), getattr(r, k + kind + "_sem")
        return (kind if kind != "s" else "space", lambda j: send, recv, sems)

    def table_start(kind, k, value):
        args = table_args(kind, k)
        getattr(r, k + kind + "_send")[...] = value
        args[2][groups[args[0]][1]] = value
        start_all(*args)

    def table_sum(kind, k):
        args = table_args(kind, k)
        wait_all(*args)
        value = args[2][0]
        for j in range(1, groups[args[0]][0]):
            value = value + args[2][j]
        return value

    r.dk_t[...] = jnp.zeros_like(r.dk_t)
    r.dv_t[...] = jnp.zeros_like(r.dv_t)

    def attend_back(d, carry):
        j = (sp + d) % ns

        @pl.when(d > 0)
        def _():
            wait_from(*do, j)

        weights = r.prob[j]
        grad_out = r.do_recv[j]
        dw = dot(grad_out, r.v_ref[...], NT)
        ds = weights * (dw - jnp.sum(dw * weights, axis=-1, keepdims=True)) * scaling
        ds = ds.astype(BF)
        r.dq[j] = dot(ds, r.k_ref[...])
        r.dv_t[...] += dot(grad_out, weights.astype(BF), TN)
        r.dk_t[...] += dot(r.q_ref[j], ds, TN)
        return carry

    lax.fori_loop(0, ns, attend_back, 0)
    for j in range(ns):
        dk = r.dk_t[:, toks * j : toks * (j + 1)].T
        dv = r.dv_t[:, toks * j : toks * (j + 1)].T
        packed = jnp.concatenate(
            [r.dq[j], dk, dv, jnp.zeros((toks, 256 - 3 * hd), F32)], axis=1
        )
        r.gp_send[j] = packed.astype(BF)
    r.gp_recv[sp] = r.gp_send[sp]
    gp = ("space", lambda j: r.gp_send.at[j], r.gp_recv, r.gp_sem)
    start_all(*gp)

    rs_y(1)
    rs_x(0)
    table_start("s", "e", to_lines([shift_t, scale_t, gate_t, gate_s], 16))
    wait_all(*mx)
    r.mixed[...] = from_blocks(r.mix_recv[...], width).astype(BF)

    wait_all(*gp)
    for h in range(heads):
        block = r.gp_recv[h].astype(F32)
        project_back(
            h, block[:, :hd], block[:, hd : 2 * hd], block[:, 2 * hd : 3 * hd], r.raw_s, r.gn_s
        )
    grad_shifted = dot(r.grw[...].astype(BF), r.wqs[...], NT)
    normed, inv_s = norm(r.tok[...].astype(F32))
    grad_in, shift_s, scale_s = modulate_back(grad_shifted, normed, inv_s, table_s)
    table_start("s", "l", to_lines([shift_s, scale_s], 8))
    r.tgrad[...] = (r.grad_mid[...] + grad_in).astype(BF)
    rs_x(1)
    rs_z(0)
    table_start("x", "e", table_sum("s", "e"))
    table_start("x", "l", table_sum("s", "l"))
    rs_z(1)
    table_start("z", "e", table_sum("x", "e"))
    table_start("z", "l", table_sum("x", "l"))
    rs_end(0, r.got)
    rs_end(1, r.gos)
    early = table_sum("z", "e")
    late = table_sum("z", "l")
    rows = [from_lines(late, 0), from_lines(late, 1), from_lines(early, 3)]
    rows += [from_lines(early, 0), from_lines(early, 1), from_lines(early, 2)]
    for i in range(6):
        r.tabs[i : i + 1, :] = rows[i]

    for args in (ps, ct, at, md, gm, mx, do, gp):
        wait_sent(*args)
    for a in range(2):
        pair_copy(a).wait_send()
        for kind in ("y", "x", "z"):
            wait_sent(*rs_args(kind, a))
    for k in ("e", "l"):
        for kind in ("s", "x", "z"):
            wait_sent(*table_args(kind, k))


def solution(mesh):
    nt, ns = mesh.shape["tm"], mesh.shape["space"]

    def on_device(
        tokens, validity, table_space, qkv_space, gains_space, out_space,
        table_time, qkv_time, gains_time, out_time, cotangent,
    ):
        z = Sizes()
        z.width = tokens.shape[3]
        z.toks = tokens.shape[2]
        z.hd = gains_space.shape[1]
        z.heads = out_space.shape[0] // z.hd
        z.ns, z.nt, z.nz = ns, nt, nt // 2
        z.cut = 640
        z.rows = 80
        heads, hd, width, toks, nz = z.heads, z.hd, z.width, z.toks, z.nz
        qw = 3 * heads * hd
        dma = pltpu.SemaphoreType.DMA
        vm = pltpu.VMEM
        third = width // 3
        scratch = {
            "wqs": vm((width, qw), BF),
            "wos": vm((heads * hd, width), BF),
            "wqt": vm((width, qw), BF),
            "wot": vm((heads * hd, width), BF),
            "w_sem": dma((4,)),
            "raw_s": vm((toks, qw), F32),
            "raw_t": vm((toks, qw), F32),
            "grw": vm((toks, qw), F32),
            "q_ref": vm((ns, toks, hd), BF),
            "k_ref": vm((ns * toks, hd), BF),
            "v_ref": vm((ns * toks, hd), BF),
            "prob": vm((ns, toks, ns * toks), F32),
            "dq": vm((ns, toks, hd), F32),
            "dk_t": vm((hd, ns * toks), F32),
            "dv_t": vm((hd, ns * toks), F32),
            "att_f": vm((toks, heads * hd), F32),
            "att_s": vm((toks, heads * hd), BF),
            "branch_s": vm((toks, width), F32),
            "grad_att": vm((toks, heads * hd), F32),
            "grad_mid": vm((toks, width), F32),
            "gb_t": vm((toks, width), BF),
            "gb_s": vm((toks, width), BF),
            "part": vm((2, 2, ns // 2, z.rows, width), BF),
            "pair_recv": vm((2, ns // 2, z.rows, width), BF),
            "pair_sem": dma((2, 2)),
        }

        def both(name, n, shape, dtype):
            scratch[name + "_send"] = vm((n,) + shape, dtype)
            scratch[name + "_recv"] = vm((n,) + shape, dtype)
            scratch[name + "_sem"] = dma((2, n))

        both("ps", ns, (toks, 256), BF)
        both("gp", ns, (toks, 256), BF)
        both("at", ns, (toks, hd), BF)
        both("do", ns, (toks, hd), BF)
        for name in ("cot", "mid", "gm", "mix"):
            both(name, nt, (16, z.cut), BF)
        for name, n, w in (("y", ns // 2, width), ("x", 4, width // 4), ("z", nz, width // 4 // nz)):
            scratch[name + "_send"] = vm((2, n, z.rows, w), BF)
            scratch[name + "_recv"] = vm((2, n, z.rows, w), BF)
            scratch[name + "_sem"] = dma((2, 2, n))
        for k, lines in (("e", 16), ("l", 8)):
            for kind, n in (("s", ns), ("x", 4), ("z", nz)):
                scratch[k + kind + "_send"] = vm((lines, third), F32)
                scratch[k + kind + "_recv"] = vm((n, lines, third), F32)
                scratch[k + kind + "_sem"] = dma((2, n))

        ins = ["tok", "cot", "val", "tab_s", "gn_s", "tab_t", "gn_t", "qkv_s", "out_s", "qkv_t", "out_t"]
        outs = ["mixed", "tgrad", "gos", "got", "tabs"]
        vmem = pl.BlockSpec(memory_space=pltpu.VMEM)
        anywhere = pl.BlockSpec(memory_space=pl.ANY)
        mixed, tgrad, gos, got, tabs = pl.pallas_call(
            functools.partial(kernel, z, ins + outs + list(scratch)),
            out_shape=[
                jax.ShapeDtypeStruct((toks, width), BF),
                jax.ShapeDtypeStruct((toks, width), BF),
                jax.ShapeDtypeStruct((hd, width // 4 // nz), F32),
                jax.ShapeDtypeStruct((hd, width // 4 // nz), F32),
                jax.ShapeDtypeStruct((6, width), F32),
            ],
            in_specs=[vmem] * 7 + [anywhere] * 4,
            out_specs=[vmem] * 5,
            scratch_shapes=list(scratch.values()),
            compiler_params=pltpu.CompilerParams(
                collective_id=0, has_side_effects=True, vmem_limit_bytes=56 * 1024 * 1024
            ),
        )(
            tokens.reshape(toks, width),
            cotangent.reshape(toks, width),
            validity.reshape(ns, toks),
            table_space,
            gains_space,
            table_time,
            gains_time,
            qkv_space,
            out_space,
            qkv_time,
            out_time,
        )
        shape = tokens.shape
        return mixed.reshape(shape), tgrad.reshape(shape), gos, got, tabs.reshape(2, 3, width)

    spread = P("dp", "tm", "space", None)
    return jax.shard_map(
        on_device,
        mesh=mesh,
        in_specs=(spread,) + (P(),) * 9 + (spread,),
        out_specs=(spread, spread, P("space", ("dp", "tm")), P("space", ("dp", "tm")), P()),
        check_vma=False,
    )
```

profile of v0, /device:TPU:32, one launch (start us, length us, event | category | flops | bytes accessed | tf_op | source)
XLA Modules:
  0.0 132.1 jit_solution(15538408434674741370)
XLA Ops:
  0.6 6.4 %copy.21.refs_7_ = bf16[1152,1728]{1,0:T(8,128)(2,1)} copy(bf16[1152,1728]{0,1:T(8,128)(2,1)} %param.14) | data formatting | bytes 7962624 | tf_op args[3]
  7.1 6.4 %copy.22.refs_9_ = bf16[1152,1728]{1,0:T(8,128)(2,1)} copy(bf16[1152,1728]{0,1:T(8,128)(2,1)} %param.18) | data formatting | bytes 7962624 | tf_op args[7]
  13.5 110.8 %shard_map.146 = (bf16[128,1152]{1,0:T(8,128)(2,1)}, bf16[128,1152]{1,0:T(8,128)(2,1)}, f32[72,36]{1,0:T(8,128)}, f32[72,36]{1,0:T(8,128)}, f32[6,1152]{1,0:T(8,128)}) custom-call(bf16[128,1152]{1,0:T(8,128)(2,1)} %bitcast.5, bf16[128,1152]{1,0:T(8,128)(2,1)} %bitcast.6, s32[8,128]{1,0:T(8,128)} %bitcast.9, f32[3,1152]{1,0:T(4,128)} %refs_3_.1, ...), custom_call_target="tpu_custom_call" | custom-call | tf_op jit(solution)/shard_map/pallas_call | solution.py:566
  124.3 1.5 %copy.23 = f32[72,36]{0,1:T(8,128)} copy(f32[72,36]{1,0:T(8,128)} %get-tuple-element.22) | data formatting | bytes 20736
  125.8 1.5 %copy.24 = f32[72,36]{0,1:T(8,128)} copy(f32[72,36]{1,0:T(8,128)} %get-tuple-element.23) | data formatting | bytes 20736
  127.3 0.8 reshape.33
  128.0 0.6 copy.25
  128.7 1.7 %copy.28 = bf16[1,1,128,1152]{3,2,1,0:T(8,128)(2,1)} copy(bf16[1,1,128,1152]{3,2,1,0:T(8,128)(2,1)} %bitcast.8) | data formatting | bytes 589824
  130.4 1.7 %copy.29 = bf16[1,1,128,1152]{3,2,1,0:T(8,128)(2,1)} copy(bf16[1,1,128,1152]{3,2,1,0:T(8,128)(2,1)} %bitcast.7) | data formatting | bytes 589824
where the time goes:
time: 133 us; the launch traced here: 132 us
  Pallas kernels  111 us (83%)
  local copies, waits for them, and re-layouts  20.6 us (15%)
    pallas_call x1, Pallas kernels, on_device(): pl.pallas_call(functools.partial(kernel, z, ins + outs + list(scratch)),...  111 us
    unnamed x7, local copies, waits for them, and re-layouts  19.8 us

commit v1 on v0

v1 whole, which is shorter than its diff:
```python
import functools

import jax
import jax.numpy as jnp
from jax import lax
from jax.experimental import pallas as pl
from jax.experimental.pallas import tpu as pltpu
from jax.sharding import PartitionSpec as P

MESH = pl.DeviceIdType.MESH
BF = jnp.bfloat16
F32 = jnp.float32
EPSILON = 1e-6
LOG2E = 1.4426950408889634

NN = (((1,), (0,)), ((), ()))
NT = (((1,), (1,)), ((), ()))
TN = (((0,), (0,)), ((), ()))


def dot(a, b, dims=NN):
    return lax.dot_general(a, b, dims, preferred_element_type=F32)


def mean(v):
    return jnp.mean(v, axis=-1, keepdims=True)


def norm(values):
    centred = values - mean(values)
    inv_std = lax.rsqrt(mean(centred * centred) + EPSILON)
    return centred * inv_std, inv_std


def feature_mean(v):
    return jnp.mean(v, axis=-2, keepdims=True)


def rms_scale(raw):
    return lax.rsqrt(feature_mean(raw * raw) + EPSILON)


def rms_back(grad, raw):
    inv = rms_scale(raw)
    return inv * (grad - raw * (inv * inv) * feature_mean(grad * raw))


def modulate_back(grad, normed, inv_std, table):
    grad_norm = grad * (1.0 + table[1:2, :])
    grad_in = inv_std * (grad_norm - mean(grad_norm) - normed * mean(grad_norm * normed))
    shift = jnp.sum(grad, axis=0, keepdims=True)
    scale = jnp.sum(grad * normed, axis=0, keepdims=True)
    return grad_in, shift, scale


class Sizes:
    pass


def to_blocks(rows, cut):
    n, width = rows.shape[0] // 8, rows.shape[1]
    cube = rows.reshape(n, 8, width)
    low = jnp.concatenate([cube[:, :, cut:], jnp.zeros((n, 8, 2 * cut - width), F32)], axis=2)
    return jnp.concatenate([cube[:, :, :cut], low], axis=1).astype(BF)


def from_blocks(blocks, width):
    n, _, cut = blocks.shape
    cube = blocks.astype(F32)
    full = jnp.concatenate([cube[:, :8, :], cube[:, 8:, : width - cut]], axis=2)
    return full.reshape(n * 8, width)


def to_lines(rows, lines):
    third = rows[0].shape[1] // 3
    parts = [r[:, third * c : third * (c + 1)] for r in rows for c in range(3)]
    if lines > len(parts):
        parts.append(jnp.zeros((lines - len(parts), third), F32))
    return jnp.concatenate(parts, axis=0)


def from_lines(lines, r):
    return jnp.concatenate([lines[3 * r + c : 3 * r + c + 1, :] for c in range(3)], axis=1)


def kernel(z, names, *refs):
    r = Sizes()
    for name, ref in zip(names, refs):
        setattr(r, name, ref)
    heads, hd, width, toks, ns, nt, nz, cut = (
        z.heads, z.hd, z.width, z.toks, z.ns, z.nt, z.nz, z.cut,
    )
    att_w = heads * hd
    hp, pair_w, np_, two = z.hp, 6 * hd, heads // 2, 2 * toks
    scaling = hd ** (-0.5)
    power = scaling * LOG2E
    dp = lax.axis_index("dp")
    tm = lax.axis_index("tm")
    sp = lax.axis_index("space")
    core, y = sp % 2, sp // 2
    x_lo, zz = tm // nz, tm % nz
    x = dp * 2 + x_lo
    nx = 4
    ny = ns // 2

    scope = []

    def phase(name):
        while scope:
            scope.pop().__exit__(None, None, None)
        if name:
            scope.append(jax.named_scope(name))
            scope[-1].__enter__()

    def remote(src, dst, send_sem, recv_sem, device):
        return pltpu.make_async_remote_copy(
            src_ref=src, dst_ref=dst, send_sem=send_sem, recv_sem=recv_sem,
            device_id=device, device_id_type=MESH,
        )

    groups = {
        "space": (ns, sp, lambda j: (dp, tm, j)),
        "tm": (nt, tm, lambda j: (dp, j, sp)),
        "y": (ny, y, lambda j: (dp, tm, j * 2 + core)),
        "x": (nx, x, lambda j: (j // 2, (j % 2) * nz + zz, sp)),
        "z": (nz, zz, lambda j: (dp, x_lo * nz + j, sp)),
    }

    def exchange(group, src_of, recv, sems, d):
        n, me, device = groups[group]
        j = (me + d) % n
        return remote(src_of(j), recv.at[me], sems.at[0, d], sems.at[1, me], device(j))

    def start_all(group, src_of, recv, sems):
        n = groups[group][0]

        def body(d, carry):
            exchange(group, src_of, recv, sems, d).start()
            return carry

        lax.fori_loop(1, n, body, 0)

    def start_to(args, j):
        n, me, _ = groups[args[0]]

        @pl.when(j != me)
        def _():
            exchange(*args, (j - me + n) % n).start()

    def wait_from(group, src_of, recv, sems, j):
        n, me, device = groups[group]
        remote(src_of(j), recv.at[j], sems.at[0, 0], sems.at[1, j], device(j)).wait_recv()

    def wait_other(args, j):
        @pl.when(j != groups[args[0]][1])
        def _():
            wait_from(*args, j)

    def wait_all(group, src_of, recv, sems):
        n, me, _ = groups[group]

        def body(d, carry):
            wait_from(group, src_of, recv, sems, (me + n - d) % n)
            return carry

        lax.fori_loop(1, n, body, 0)

    def wait_sent(group, src_of, recv, sems):
        n = groups[group][0]

        def body(d, carry):
            exchange(group, src_of, recv, sems, d).wait_send()
            return carry

        lax.fori_loop(1, n, body, 0)

    phase("greet")
    pair_order = [(y + d) % np_ for d in range(1, np_ + 1)]

    def rows_of(b):
        return pl.ds(pl.multiple_of(b * pair_w, pair_w), pair_w)

    pair_copies = [
        pltpu.make_async_copy(r.qkv_s.at[rows_of(b)], r.wqs.at[rows_of(b)], r.q_sem.at[i])
        for i, b in enumerate(pair_order)
    ]
    cot_copy, wos_copy, wot_copy, wqt_copy = [
        pltpu.make_async_copy(src, dst, r.w_sem.at[i])
        for i, (src, dst) in enumerate(
            [(r.cot, r.cot_v), (r.out_s, r.wos), (r.out_t, r.wot), (r.qkv_t, r.wqt)]
        )
    ]
    for copy in pair_copies + [cot_copy, wos_copy, wot_copy, wqt_copy]:
        copy.start()
    barrier = pltpu.get_barrier_semaphore()

    def signal(device):
        pl.semaphore_signal(barrier, inc=1, device_id=device, device_id_type=MESH)

    def greet(group):
        n, me, device = groups[group]

        def body(d, carry):
            signal(device((me + d) % n))
            return carry

        lax.fori_loop(1, n, body, 0)

    greet("space")
    greet("tm")
    other = 1 - dp
    signal((other, tm, sp))
    signal((other, (1 - x_lo) * nz + zz, sp))

    phase("norm_space")
    tokens = r.tok[...].astype(F32)
    table_s = r.tab_s[...]
    normed, _ = norm(tokens)
    shifted = (normed * (1.0 + table_s[1:2, :]) + table_s[0:1, :]).astype(BF)
    r.shift_s[...] = shifted

    def gain_columns(ref):
        g = ref[...]
        return [jnp.broadcast_to(g[i : i + 1, :], (toks, hd)).T for i in range(2)]

    gain_s = gain_columns(r.gn_s)
    gain_t = gain_columns(r.gn_t)
    pad_rows = jnp.zeros((hp - hd, toks), F32)
    first_row = lax.broadcasted_iota(jnp.int32, (hp - hd, toks), 0) == 0

    def padded(part):
        return jnp.concatenate([part, pad_rows], axis=0)

    phase("wait_barrier")
    pl.semaphore_wait(barrier, ns - 1 + nt - 1 + 2)
    phase("project_space")
    ps = ("space", lambda j: r.ps_send.at[j], r.ps_recv, r.ps_sem)
    for i, b in enumerate(pair_order):
        pair_copies[i].wait()
        raw = dot(r.wqs[rows_of(b), :], r.shift_s[...], NT)
        r.raw_s[b] = raw
        cube = raw.reshape(6, hd, toks)
        for c in range(2):
            p0, p1, p2 = cube[3 * c], cube[3 * c + 1], cube[3 * c + 2]
            q = p0 * rms_scale(p0) * gain_s[0]
            k = p1 * rms_scale(p1) * gain_s[1]
            r.ps_send[2 * b + c] = jnp.concatenate([q, k, p2, pad_rows], axis=0).astype(BF)
            start_to(ps, 2 * b + c)
    r.ps_recv[sp] = r.ps_send[sp]

    phase("masks")
    own_row = r.val[pl.ds(sp, 1), :].astype(F32)
    row_id = lax.broadcasted_iota(jnp.int32, (toks, toks), 0)
    col_id = lax.broadcasted_iota(jnp.int32, (toks, toks), 1)
    own = jnp.broadcast_to(own_row, (toks, toks))
    mask_s = jnp.sum(jnp.where(row_id == col_id, own, 0.0), axis=1, keepdims=True)
    mask_t = jnp.sum(jnp.where(tm * 8 + row_id % 8 == col_id, own, 0.0), axis=1, keepdims=True)
    cot_copy.wait()
    r.cot_send[...] = to_blocks(r.cot_v[...].astype(F32), cut)
    r.cot_recv[tm] = r.cot_send[tm]
    ct = ("tm", lambda j: r.cot_send.at[j], r.cot_recv, r.cot_sem)

    phase("unpack_packed")

    def unpack(d, carry):
        j = (sp + ns - d) % ns
        wait_other(ps, j)
        block = r.ps_recv[j].astype(F32)
        at = pl.ds(pl.multiple_of(j * toks, toks), toks)
        keys, values = block[hd : 2 * hd, :], block[2 * hd : 3 * hd, :]
        bias = jnp.where(r.val[pl.ds(j, 1), :] > 0, 0.0, -1e30)
        r.q_t[:, at] = jnp.concatenate([block[:hd, :], jnp.where(first_row, 1.0, 0.0)], axis=0).astype(BF)
        r.k_t[:, at] = padded(keys).astype(BF)
        r.v_t[:, at] = padded(values).astype(BF)
        r.k_ref[at, :] = jnp.concatenate([keys, jnp.where(first_row, bias, 0.0)], axis=0).T.astype(BF)
        r.v_ref[at, :] = padded(values).T.astype(BF)
        return carry

    lax.fori_loop(0, ns, unpack, 0)
    start_all(*ct)

    at = ("space", lambda j: r.at_send.at[j], r.at_recv, r.at_sem)

    def two_of(b):
        return pl.ds(pl.multiple_of(b * two, two), two)

    phase("attend_space")
    for b in pair_order:
        scores = dot(r.k_ref[...], r.q_t[:, two_of(b)])
        top = jnp.max(scores, axis=0, keepdims=True)
        exps = jnp.exp2(scores * power - top * power)
        inverse = 1.0 / jnp.sum(exps, axis=0, keepdims=True)
        exps = exps.astype(BF)
        r.prob[b] = exps
        out = dot(r.v_t[...], exps) * inverse
        r.inverse[b] = inverse
        r.o_ref[b] = out
        for c in range(2):
            r.at_send[2 * b + c] = out[:, toks * c : toks * (c + 1)].astype(BF)
            start_to(at, 2 * b + c)
    r.at_recv[sp] = r.at_send[sp]
    phase("wait_attended")
    wait_all(*at)
    phase("out_space")
    att_s = jnp.concatenate([r.at_recv[h].astype(F32)[:hd, :] for h in range(heads)], axis=0).astype(BF)
    r.att_s[...] = att_s
    wos_copy.wait()
    branch_s = dot(att_s, r.wos[...], TN)
    r.branch_s[...] = branch_s
    middle = r.tok[...].astype(F32) + mask_s * table_s[2:3, :] * branch_s
    r.mid_send[...] = to_blocks(middle, cut)
    r.mid_recv[tm] = r.mid_send[tm]
    md = ("tm", lambda j: r.mid_send.at[j], r.mid_recv, r.mid_sem)
    start_all(*md)

    phase("wait_cotangent")
    table_t = r.tab_t[...]
    wait_all(*ct)
    phase("grad_branch_time")
    masked = from_blocks(r.cot_recv[...], width) * mask_t
    grad_branch = (masked * table_t[2:3, :]).astype(BF)
    r.gb_t[...] = grad_branch
    wot_copy.wait()
    r.grad_att[...] = dot(r.wot[...], grad_branch, NT)
    wqt_copy.wait()
    for args in (ps, at, ct):
        wait_sent(*args)

    phase("wait_middle")
    wait_all(*md)
    phase("norm_time")
    normed, _ = norm(from_blocks(r.mid_recv[...], width))
    shifted = (normed * (1.0 + table_t[1:2, :]) + table_t[0:1, :]).astype(BF)
    phase("project_time")
    raw = dot(r.wqt[...], shifted, NT).reshape(heads, 3, hd, toks)
    p0, p1, p2 = raw[:, 0], raw[:, 1], raw[:, 2]
    s0, s1 = rms_scale(p0), rms_scale(p1)
    r.p0[...] = p0
    r.p1[...] = p1
    q = p0 * s0 * gain_t[0][None]
    k = p1 * s1 * gain_t[1][None]
    q_f = [padded(q[h]) for h in range(heads)]
    k_f = [padded(k[h]) for h in range(heads)]
    v_f = [padded(p2[h]) for h in range(heads)]
    q_t, k_t, v_t = ([v.astype(BF) for v in part] for part in (q_f, k_f, v_f))
    phase("attend_time")
    same = (row_id % 8 == col_id % 8)[None]
    scores = jnp.stack([dot(k_f[h].T.astype(BF), q_t[h]) for h in range(heads)], axis=0)
    scores = jnp.where(same, scores, -1e30)
    exps = jnp.exp2((scores - jnp.max(scores, axis=1, keepdims=True)) * power)
    weights = exps * (1.0 / jnp.sum(exps, axis=1, keepdims=True))
    rounded = weights.astype(BF)
    att = jnp.concatenate([dot(v_t[h], rounded[h])[:hd, :] for h in range(heads)], axis=0)
    r.att_t[...] = att.astype(BF)
    phase("attend_back_time")
    do_t = [padded(r.grad_att[hd * h : hd * (h + 1), :]).astype(BF) for h in range(heads)]
    dw = jnp.stack([dot(v_f[h].T.astype(BF), do_t[h]) for h in range(heads)], axis=0)
    ds = weights * (dw - jnp.sum(dw * weights, axis=1, keepdims=True)) * scaling
    ds = ds.astype(BF)

    def stacked(parts):
        return jnp.stack([v[:hd, :] for v in parts], axis=0).astype(BF).astype(F32)

    dq = stacked([dot(k_t[h], ds[h]) for h in range(heads)])
    dk = stacked([dot(q_t[h], ds[h], NT) for h in range(heads)])
    dv = stacked([dot(do_t[h], rounded[h], NT) for h in range(heads)])
    phase("rms_back_time")
    dq = rms_back(dq * gain_t[0][None], r.p0[...])
    dk = rms_back(dk * gain_t[1][None], r.p1[...])
    grad_raw = jnp.stack([dq, dk, dv], axis=1).reshape(3 * att_w, toks).astype(BF)
    phase("back_time")
    grad_shifted = dot(grad_raw, r.wqt[...], TN)
    normed, inv_t = norm(from_blocks(r.mid_recv[...], width))
    grad_in, shift_t, scale_t = modulate_back(grad_shifted, normed, inv_t, table_t)
    r.gm_send[...] = to_blocks(from_blocks(r.cot_recv[...], width) + grad_in, cut)
    r.gm_recv[tm] = r.gm_send[tm]
    gm = ("tm", lambda j: r.gm_send.at[j], r.gm_recv, r.gm_sem)
    start_all(*gm)

    pair = (dp, tm, sp + 1 - 2 * core)

    def pair_copy(a):
        return remote(
            r.part.at[a, 1 - core], r.pair_recv.at[a], r.pair_sem.at[0, a], r.pair_sem.at[1, a], pair
        )

    def partial_grad(a, att, grad_branch):
        full = dot(att, grad_branch)
        pad = jnp.zeros((hp - hd, width), F32)
        for h in range(heads):
            block = jnp.concatenate([full[hd * h : hd * (h + 1), :], pad], axis=0)
            r.part[a, h % 2, h // 2] = block.astype(BF)
        pair_copy(a).start()

    def rs_args(kind, a):
        send, recv, sems = {
            "y": (r.y_send, r.y_recv, r.y_sem),
            "x": (r.x_send, r.x_recv, r.x_sem),
            "z": (r.z_send, r.z_recv, r.z_sem),
        }[kind]
        return (kind, lambda j: send.at[a, j], recv.at[a], sems.at[a])

    def rs_y(a):
        pair_copy(a).wait_recv()
        r.y_send[a] = (r.part[a, core].astype(F32) + r.pair_recv[a].astype(F32)).astype(BF)
        r.y_recv[a, y] = r.y_send[a, y]
        start_all(*rs_args("y", a))

    def total(ref, a, n):
        value = ref[a, 0].astype(F32)
        for j in range(1, n):
            value = value + ref[a, j].astype(F32)
        return value

    def rs_x(a):
        wait_all(*rs_args("y", a))
        value = total(r.y_recv, a, ny)
        part_w = width // nx
        for j in range(nx):
            r.x_send[a, j] = value[:, part_w * j : part_w * (j + 1)].astype(BF)
        r.x_recv[a, x] = r.x_send[a, x]
        start_all(*rs_args("x", a))

    def rs_z(a):
        wait_all(*rs_args("x", a))
        value = total(r.x_recv, a, nx)
        part_w = width // nx // nz
        for j in range(nz):
            r.z_send[a, j] = value[:, part_w * j : part_w * (j + 1)].astype(BF)
        r.z_recv[a, zz] = r.z_send[a, zz]
        start_all(*rs_args("z", a))

    def rs_end(a, out_ref):
        wait_all(*rs_args("z", a))
        out_ref[...] = total(r.z_recv, a, nz)[:hd, :].T

    def table_args(kind, k):
        send, recv, sems = (getattr(r, k + kind + end) for end in ("_send", "_recv", "_sem"))
        return (kind if kind != "s" else "space", lambda j: send, recv, sems)

    def table_start(kind, k, value):
        args = table_args(kind, k)
        getattr(r, k + kind + "_send")[...] = value
        args[2][groups[args[0]][1]] = value
        start_all(*args)

    def table_sum(kind, k):
        args = table_args(kind, k)
        wait_all(*args)
        value = args[2][0]
        for j in range(1, groups[args[0]][0]):
            value = value + args[2][j]
        return value

    phase("partial_time")
    partial_grad(0, r.att_t[...], r.gb_t[...])
    phase("branch_time")
    branch_t = dot(r.att_t[...], r.wot[...], TN)
    middle = from_blocks(r.mid_recv[...], width)
    r.mix_send[...] = to_blocks(middle + mask_t * table_t[2:3, :] * branch_t, cut)
    r.mix_recv[tm] = r.mix_send[tm]
    mx = ("tm", lambda j: r.mix_send.at[j], r.mix_recv, r.mix_sem)
    gate_t = jnp.sum(from_blocks(r.cot_recv[...], width) * mask_t * branch_t, axis=0, keepdims=True)
    phase("pair_time")
    rs_y(0)
    wait_sent(*md)

    phase("wait_grad_middle")
    wait_all(*gm)
    phase("grad_branch_space")
    grad_mid = from_blocks(r.gm_recv[...], width)
    r.grad_mid[...] = grad_mid
    masked = grad_mid * mask_s
    grad_branch = (masked * table_s[2:3, :]).astype(BF)
    r.gb_s[...] = grad_branch
    grad_att = dot(r.wos[...], grad_branch, NT)
    for h in range(heads):
        r.do_send[h] = padded(grad_att[hd * h : hd * (h + 1), :]).astype(BF)
    r.do_recv[sp] = r.do_send[sp]
    do = ("space", lambda j: r.do_send.at[j], r.do_recv, r.do_sem)
    start_all(*do)
    start_all(*mx)
    phase("partial_space")
    partial_grad(1, r.att_s[...], r.gb_s[...])
    gate_s = jnp.sum(r.grad_mid[...] * mask_s * r.branch_s[...], axis=0, keepdims=True)
    table_start("s", "e", to_lines([shift_t, scale_t, gate_t, gate_s], 16))
    phase("rs_x0")
    rs_x(0)

    dqs = ("space", lambda j: r.dq_send.at[j], r.dq_recv, r.dq_sem)
    dks = ("space", lambda j: r.dk_send.at[j], r.dk_recv, r.dk_sem)
    back_order = [(y + np_ - d) % np_ for d in range(np_)]
    for i, b in enumerate(back_order):
        phase("attend_back")
        for c in range(2):
            wait_other(do, 2 * b + c)
        grad_out = jnp.concatenate([r.do_recv[2 * b], r.do_recv[2 * b + 1]], axis=1).astype(F32)
        grad_out = (grad_out * (r.inverse[b] * scaling)).astype(BF)
        shared = jnp.sum(grad_out.astype(F32) * r.o_ref[b], axis=0, keepdims=True)
        exps = r.prob[b]
        ds = (exps.astype(F32) * (dot(r.v_ref[...], grad_out) - shared)).astype(BF)
        dq = dot(r.k_t[...], ds).astype(BF)
        for c in range(2):
            r.dq_send[2 * b + c] = dq[:, toks * c : toks * (c + 1)]
            start_to(dqs, 2 * b + c)
        dv = dot(grad_out, exps, NT)
        dk = dot(r.q_t[:, two_of(b)], ds, NT)
        r.dv_t[...] = dv if i == 0 else r.dv_t[...] + dv
        r.dk_t[...] = dk if i == 0 else r.dk_t[...] + dk
        if i == 1:
            phase("pair_space")
            rs_y(1)
    phase("pack_grads")
    for j in range(ns):
        cols = slice(toks * j, toks * (j + 1))
        r.dk_send[j] = jnp.concatenate(
            [r.dk_t[:hd, cols], r.dv_t[:hd, cols] * (1.0 / scaling)], axis=0
        ).astype(BF)
    start_all(*dks)
    r.dq_recv[sp] = r.dq_send[sp]
    r.dk_recv[sp] = r.dk_send[sp]

    phase("tables_early_x")
    table_start("x", "e", table_sum("s", "e"))
    phase("rs_z0")
    rs_z(0)
    phase("mixed")
    wait_all(*mx)
    r.mixed[...] = from_blocks(r.mix_recv[...], width).astype(BF)
    for args in (gm, do, mx):
        wait_sent(*args)
    pair_copy(0).wait_send()
    for kind in ("y", "x"):
        wait_sent(*rs_args(kind, 0))
    phase("tables_early_z")
    table_start("z", "e", table_sum("x", "e"))

    normed, inv_s = norm(r.tok[...].astype(F32))
    for i, b in enumerate(back_order):
        phase("wait_grad_packed")
        for c in range(2):
            wait_other(dqs, 2 * b + c)
            wait_other(dks, 2 * b + c)
        phase("back_space")
        raw = r.raw_s[b].reshape(6, hd, toks)
        parts = []
        for c in range(2):
            dq = r.dq_recv[2 * b + c].astype(F32)[:hd, :]
            dkv = r.dk_recv[2 * b + c].astype(F32)
            parts.append(rms_back(dq * gain_s[0], raw[3 * c]))
            parts.append(rms_back(dkv[:hd, :] * gain_s[1], raw[3 * c + 1]))
            parts.append(dkv[hd:, :])
        grad_raw = jnp.concatenate(parts, axis=0).astype(BF)
        share = dot(grad_raw, r.wqs[rows_of(b), :], TN)
        r.acc[...] = share if i == 0 else r.acc[...] + share
        if i == 0:
            phase("rs_x1")
            rs_x(1)
    phase("end_space")
    grad_in, shift_s, scale_s = modulate_back(r.acc[...], normed, inv_s, table_s)
    table_start("s", "l", to_lines([shift_s, scale_s], 8))
    r.tgrad[...] = (r.grad_mid[...] + grad_in).astype(BF)
    phase("rs_z1")
    rs_z(1)
    phase("rs_end0")
    rs_end(0, r.got)
    phase("tables_x")
    table_start("x", "l", table_sum("s", "l"))
    early = table_sum("z", "e")
    for args in (dqs, dks):
        wait_sent(*args)
    pair_copy(1).wait_send()
    for args in [rs_args("y", 1), rs_args("x", 1), rs_args("z", 0)]:
        wait_sent(*args)
    for kind in ("s", "x", "z"):
        wait_sent(*table_args(kind, "e"))
    phase("tables_z")
    table_start("z", "l", table_sum("x", "l"))
    phase("rs_end1")
    rs_end(1, r.gos)
    wait_sent(*rs_args("z", 1))
    wait_sent(*table_args("s", "l"))
    wait_sent(*table_args("x", "l"))
    phase("tables_end")
    late = table_sum("z", "l")
    space_rows = [from_lines(late, 0), from_lines(late, 1), from_lines(early, 3)]
    for i in range(3):
        r.tabs[i] = jnp.concatenate([space_rows[i], from_lines(early, i)], axis=0)
    wait_sent(*table_args("z", "l"))
    phase(None)


def hand_on(*refs):
    n = len(refs) // 2
    for i in range(n):
        refs[n + i][...] = refs[i][...]


def solution(mesh):
    nt, ns = mesh.shape["tm"], mesh.shape["space"]

    def on_device(
        tokens, validity, table_space, qkv_space, gains_space, out_space,
        table_time, qkv_time, gains_time, out_time, cotangent,
    ):
        z = Sizes()
        z.width = tokens.shape[3]
        z.toks = tokens.shape[2]
        z.hd = gains_space.shape[1]
        z.heads = out_space.shape[0] // z.hd
        z.ns, z.nt, z.nz = ns, nt, nt // 2
        z.cut = 640
        z.hp = 80
        heads, hd, width, toks, nz, hp = z.heads, z.hd, z.width, z.toks, z.nz, z.hp
        qw, pairs, patches = 3 * heads * hd, ns // 2, ns * toks
        dma = pltpu.SemaphoreType.DMA
        vm = pltpu.VMEM
        third = width // 3
        scratch = {
            "wqs": vm((qw, width), BF),
            "wos": vm((heads * hd, width), BF),
            "wqt": vm((qw, width), BF),
            "wot": vm((heads * hd, width), BF),
            "cot_v": vm((toks, width), BF),
            "q_sem": dma((pairs,)),
            "w_sem": dma((4,)),
            "shift_s": vm((toks, width), BF),
            "raw_s": vm((pairs, 6 * hd, toks), F32),
            "p0": vm((heads, hd, toks), F32),
            "p1": vm((heads, hd, toks), F32),
            "q_t": vm((hp, patches), BF),
            "k_t": vm((hp, patches), BF),
            "v_t": vm((hp, patches), BF),
            "k_ref": vm((patches, hp), BF),
            "v_ref": vm((patches, hp), BF),
            "prob": vm((pairs, patches, 2 * toks), BF),
            "inverse": vm((pairs, 1, 2 * toks), F32),
            "o_ref": vm((pairs, hp, 2 * toks), F32),
            "dk_t": vm((hp, patches), F32),
            "dv_t": vm((hp, patches), F32),
            "att_s": vm((heads * hd, toks), BF),
            "att_t": vm((heads * hd, toks), BF),
            "branch_s": vm((toks, width), F32),
            "grad_att": vm((heads * hd, toks), F32),
            "grad_mid": vm((toks, width), F32),
            "acc": vm((toks, width), F32),
            "gb_t": vm((toks, width), BF),
            "gb_s": vm((toks, width), BF),
            "part": vm((2, 2, pairs, hp, width), BF),
            "pair_recv": vm((2, pairs, hp, width), BF),
            "pair_sem": dma((2, 2)),
        }

        def both(name, n, shape, dtype):
            scratch[name + "_send"] = vm((n,) + shape, dtype)
            scratch[name + "_recv"] = vm((n,) + shape, dtype)
            scratch[name + "_sem"] = dma((2, n))

        both("ps", ns, (3 * hd + 8, toks), BF)
        both("dq", ns, (hp, toks), BF)
        both("dk", ns, (2 * hd, toks), BF)
        both("at", ns, (hp, toks), BF)
        both("do", ns, (hp, toks), BF)
        for name in ("cot", "mid", "gm", "mix"):
            both(name, nt, (16, z.cut), BF)
        for name, n, w in (("y", pairs, width), ("x", 4, width // 4), ("z", nz, width // 4 // nz)):
            scratch[name + "_send"] = vm((2, n, hp, w), BF)
            scratch[name + "_recv"] = vm((2, n, hp, w), BF)
            scratch[name + "_sem"] = dma((2, 2, n))
        for k, lines in (("e", 16), ("l", 8)):
            for kind, n in (("s", ns), ("x", 4), ("z", nz)):
                scratch[k + kind + "_send"] = vm((lines, third), F32)
                scratch[k + kind + "_recv"] = vm((n, lines, third), F32)
                scratch[k + kind + "_sem"] = dma((2, n))

        ins = ["tok", "cot", "val", "tab_s", "gn_s", "tab_t", "gn_t", "qkv_s", "out_s", "qkv_t", "out_t"]
        outs = ["mixed", "tgrad", "gos", "got", "tabs"]
        vmem = pl.BlockSpec(memory_space=pltpu.VMEM)
        anywhere = pl.BlockSpec(memory_space=pl.ANY)
        results = pl.pallas_call(
            functools.partial(kernel, z, ins + outs + list(scratch)),
            out_shape=[
                jax.ShapeDtypeStruct((toks, width), BF),
                jax.ShapeDtypeStruct((toks, width), BF),
                jax.ShapeDtypeStruct((width // 4 // nz, hd), F32),
                jax.ShapeDtypeStruct((width // 4 // nz, hd), F32),
                jax.ShapeDtypeStruct((3, 2, width), F32),
            ],
            in_specs=[vmem] + [anywhere] + [vmem] * 5 + [anywhere] * 4,
            out_specs=[vmem] * 5,
            scratch_shapes=list(scratch.values()),
            compiler_params=pltpu.CompilerParams(
                collective_id=0, has_side_effects=True, vmem_limit_bytes=56 * 1024 * 1024
            ),
        )(
            tokens.reshape(toks, width),
            cotangent.reshape(toks, width),
            validity.reshape(ns, toks),
            table_space,
            gains_space,
            table_time,
            gains_time,
            qkv_space.T,
            out_space,
            qkv_time.T,
            out_time,
        )
        mixed, tgrad, gos, got, tabs = pl.pallas_call(
            hand_on,
            out_shape=[jax.ShapeDtypeStruct(v.shape, v.dtype) for v in results],
            in_specs=[vmem] * 5,
            out_specs=[vmem] * 5,
        )(*results)
        shape = tokens.shape
        return mixed.reshape(shape), tgrad.reshape(shape), gos.T, got.T, tabs.transpose(1, 0, 2)

    spread = P("dp", "tm", "space", None)
    return jax.shard_map(
        on_device,
        mesh=mesh,
        in_specs=(spread,) + (P(),) * 9 + (spread,),
        out_specs=(spread, spread, P("space", ("dp", "tm")), P("space", ("dp", "tm")), P()),
        check_vma=False,
    )
```

time: 133 us -> 95.6 us (0.72)
  local copies, waits for them, and re-layouts: 20.6 us -> 0 us
  Pallas kernels: 111 us -> 93.6 us
    unnamed x7 -> x0, local copies, waits for them, and re-layouts: 19.8 us -> none
    pallas_call x1, Pallas kernels: 111 us -> 91.7 us  [on_device(): pl.pallas_call(functools.partial(kernel, z, ins + outs + list(scratch)),...]
    pallas_call x0 -> x1, Pallas kernels: none -> 1.92 us  [on_device(): pl.pallas_call(hand_on, out_shape=[jax.ShapeDtypeStruct(v.shape, v.dtype)...]
where the time goes in v1:
time: 95.6 us; the launch traced here: 94.3 us
  Pallas kernels  93.6 us (98%)
    pallas_call x1, Pallas kernels, on_device(): pl.pallas_call(functools.partial(kernel, z, ins + outs + list(scratch)),...  91.7 us
    pallas_call x1, Pallas kernels, on_device(): pl.pallas_call(hand_on, out_shape=[jax.ShapeDtypeStruct(v.shape, v.dtype)...  1.92 us

profile of v1, /device:TPU:32, one launch (start us, length us, event | category | flops | bytes accessed | tf_op | source)
XLA Modules:
  0.0 94.3 jit_solution(4455262323856016651)
XLA Ops:
  0.6 91.7 %shard_map.146 = (bf16[128,1152]{1,0:T(8,128)(2,1)}, bf16[128,1152]{1,0:T(8,128)(2,1)}, f32[36,72]{1,0:T(8,128)}, f32[36,72]{1,0:T(8,128)}, f32[3,2,1152]{2,1,0:T(2,128)}) custom-call(bf16[128,1152]{1,0:T(8,128)(2,1)} %bitcast.12, bf16[128,1152]{1,0:T(8,128)(2,1)} %bitcast.13, s32[8,128]{1,0:T(8,128)} %bitcast.14, f32[3,1152]{1,0:T(4,128)} %refs_3_.1, ...), custom_call_target="tpu_custom_call" | custom-call | tf_op jit(solution)/shard_map/pallas_call | solution.py:680
  92.3 1.9 %shard_map.147 = (bf16[128,1152]{1,0:T(8,128)(2,1)}, bf16[128,1152]{1,0:T(8,128)(2,1)}, f32[36,72]{1,0:T(8,128)}, f32[36,72]{1,0:T(8,128)}, f32[3,2,1152]{2,1,0:T(2,128)}) custom-call(bf16[128,1152]{1,0:T(8,128)(2,1)} %get-tuple-element.15.refs_0_, bf16[128,1152]{1,0:T(8,128)(2,1)} %get-tuple-element.16.refs_1_, f32[36,72]{1,0:T(8,128)} %get-tuple-element.17.refs_2_, ...), custom_call_target="tpu_custom_call" | custom-call | tf_op jit(solution)/shard_map/pallas_call | solution.py:708

commit v2 on v1

v2 whole, which is shorter than its diff:
```python
import functools

import jax
import jax.numpy as jnp
from jax import lax
from jax.experimental import pallas as pl
from jax.experimental.pallas import tpu as pltpu
from jax.sharding import PartitionSpec as P

MESH = pl.DeviceIdType.MESH
BF = jnp.bfloat16
F32 = jnp.float32
EPSILON = 1e-6
LOG2E = 1.4426950408889634

NN = (((1,), (0,)), ((), ()))
NT = (((1,), (1,)), ((), ()))
TN = (((0,), (0,)), ((), ()))


def dot(a, b, dims=NN):
    return lax.dot_general(a, b, dims, preferred_element_type=F32)


def mean(v):
    return jnp.mean(v, axis=-1, keepdims=True)


def norm(values):
    centred = values - mean(values)
    inv_std = lax.rsqrt(mean(centred * centred) + EPSILON)
    return centred * inv_std, inv_std


def feature_mean(v):
    return jnp.mean(v, axis=-2, keepdims=True)


def rms_scale(raw):
    return lax.rsqrt(feature_mean(raw * raw) + EPSILON)


def rms_back(grad, raw):
    inv = rms_scale(raw)
    return inv * (grad - raw * (inv * inv) * feature_mean(grad * raw))


def modulate_back(grad, normed, inv_std, table):
    grad_norm = grad * (1.0 + table[1:2, :])
    grad_in = inv_std * (grad_norm - mean(grad_norm) - normed * mean(grad_norm * normed))
    shift = jnp.sum(grad, axis=0, keepdims=True)
    scale = jnp.sum(grad * normed, axis=0, keepdims=True)
    return grad_in, shift, scale


class Sizes:
    pass


def to_blocks(rows):
    n, width = rows.shape[0] // 8, rows.shape[1]
    cube = rows.reshape(n, 8, width)
    return jnp.concatenate([cube[:, :, c : c + 128] for c in range(0, width, 128)], axis=1).astype(BF)


def from_blocks(blocks):
    n, lines, _ = blocks.shape
    cube = blocks.astype(F32)
    full = jnp.concatenate([cube[:, c : c + 8, :] for c in range(0, lines, 8)], axis=2)
    return full.reshape(n * 8, lines * 16)


def to_lines(rows, lines):
    parts = [r[:, c : c + 128] for r in rows for c in range(0, rows[0].shape[1], 128)]
    if lines > len(parts):
        parts.append(jnp.zeros((lines - len(parts), 128), F32))
    return jnp.concatenate(parts, axis=0)


def from_lines(lines, r, n):
    return jnp.concatenate([lines[n * r + c : n * r + c + 1, :] for c in range(n)], axis=1)


def kernel(z, names, *refs):
    r = Sizes()
    for name, ref in zip(names, refs):
        setattr(r, name, ref)
    heads, hd, width, toks, ns, nt, nz = (
        z.heads, z.hd, z.width, z.toks, z.ns, z.nt, z.nz,
    )
    att_w = heads * hd
    hp, pair_w, np_, two = z.hp, 6 * hd, heads // 2, 2 * toks
    scaling = hd ** (-0.5)
    power = scaling * LOG2E
    dp = lax.axis_index("dp")
    tm = lax.axis_index("tm")
    sp = lax.axis_index("space")
    core, y = sp % 2, sp // 2
    sibling = sp + 1 - 2 * core
    x_lo, zz = tm // nz, tm % nz
    x = dp * 2 + x_lo
    nx = 4
    ny = ns // 2

    def remote(src, dst, send_sem, recv_sem, device):
        return pltpu.make_async_remote_copy(
            src_ref=src, dst_ref=dst, send_sem=send_sem, recv_sem=recv_sem,
            device_id=device, device_id_type=MESH,
        )

    groups = {
        "space": (ns, sp, lambda j: (dp, tm, j)),
        "tm": (nt, tm, lambda j: (dp, j, sp)),
        "y": (ny, y, lambda j: (dp, tm, j * 2 + core)),
        "x": (nx, x, lambda j: (j // 2, (j % 2) * nz + zz, sp)),
        "z": (nz, zz, lambda j: (dp, x_lo * nz + j, sp)),
    }

    def exchange(group, src_of, recv, sems, d, each=False):
        n, me, device = groups[group]
        j = (me + d) % n
        arrived = sems.at[1 + me] if each else sems.at[1]
        return remote(src_of(j), recv.at[me], sems.at[0], arrived, device(j))

    def whole(group, src_of, recv, sems, each=False):
        n, me, device = groups[group]
        part = recv.at[pl.ds(0, n - 1)]
        return remote(part, part, sems.at[0], sems.at[1], device((me + 1) % n))

    ring = [4, 3, 5, 2, 6, 1, 7]
    order = {
        "space": ring,
        "z": ring,
        "x": [2, 1, 3],
        "y": [2, 1, 3],
        "tm": [d + h for d in ring for h in (0, nz)] + [nz],
    }

    def start_all(group, src_of, recv, sems, each=False):
        for d in order[group]:
            exchange(group, src_of, recv, sems, d, each).start()

    def start_to(args, j):
        n, me, _ = groups[args[0]]
        exchange(*args[:4], (j - me + n) % n, *args[4:]).start()

    def wait_from(group, src_of, recv, sems, each, j):
        device = groups[group][2]
        remote(src_of(j), recv.at[j], sems.at[0], sems.at[1 + j], device(j)).wait_recv()

    def wait_all(*args):
        whole(*args).wait_recv()

    def wait_sent(*args):
        whole(*args).wait_send()

    barrier = pltpu.get_barrier_semaphore()

    def signal(device):
        pl.semaphore_signal(barrier, inc=1, device_id=device, device_id_type=MESH)

    def greet(group):
        n, me, device = groups[group]

        def body(d, carry):
            signal(device((me + d) % n))
            return carry

        lax.fori_loop(1, n, body, 0)

    pair_order = [(y + d) % np_ for d in (2, 1, 3, 0)]

    def rows_of(b):
        return pl.ds(pl.multiple_of(b * pair_w, pair_w), pair_w)

    results = [
        pltpu.make_async_copy(src, dst, r.o_sem.at[i])
        for i, (src, dst) in enumerate(
            [
                (r.mixed, r.mixed_out),
                (r.tgrad, r.tgrad_out),
                (r.gos, r.gos_out),
                (r.got, r.got_out),
                (r.tabs, r.tabs_out),
            ]
        )
    ]
    pair_copies = [
        pltpu.make_async_copy(r.qkv_s.at[rows_of(b)], r.wqs.at[rows_of(b)], r.q_sem.at[i])
        for i, b in enumerate(pair_order)
    ]
    copies = {
        name: pltpu.make_async_copy(src, dst, r.w_sem.at[i])
        for i, (name, src, dst) in enumerate(
            [
                ("tok", r.tok_in, r.tok),
                ("tab_s", r.tab_s_in, r.tab_s),
                ("gn_s", r.gn_s_in, r.gn_s),
                ("val", r.val_in, r.val),
                ("cot", r.cot_in, r.cot),
                ("tab_t", r.tab_t_in, r.tab_t),
                ("gn_t", r.gn_t_in, r.gn_t),
                ("wos", r.out_s, r.wos),
                ("wot", r.out_t, r.wot),
                ("wqt", r.qkv_t, r.wqt),
            ]
        )
    }
    for name in ("tok", "tab_s", "gn_s"):
        copies[name].start()
    pair_copies[0].start()
    greet("space")
    greet("tm")
    other = 1 - dp
    signal((other, tm, sp))
    signal((other, (1 - x_lo) * nz + zz, sp))
    for copy in pair_copies[1:]:
        copy.start()
    for name in ("val", "cot", "tab_t", "gn_t", "wos", "wot", "wqt"):
        copies[name].start()

    copies["tok"].wait()
    copies["tab_s"].wait()
    tokens = r.tok[...].astype(F32)
    table_s = r.tab_s[...]
    normed, _ = norm(tokens)
    shifted = (normed * (1.0 + table_s[1:2, :]) + table_s[0:1, :]).astype(BF)
    r.shift_s[...] = shifted

    def gain_columns(ref):
        g = ref[...]
        return [jnp.broadcast_to(g[i : i + 1, :], (toks, hd)).T for i in range(2)]

    copies["gn_s"].wait()
    gain_s = gain_columns(r.gn_s)
    pad_rows = jnp.zeros((hp - hd, toks), F32)
    first_row = lax.broadcasted_iota(jnp.int32, (hp - hd, toks), 0) == 0

    def padded(part):
        return jnp.concatenate([part, pad_rows], axis=0)

    kv = ("space", lambda j: r.kv_send.at[j], r.kv_recv, r.kv_sem, True)
    qs = ("space", lambda j: r.qs_send.at[j], r.qs_recv, r.qs_sem, True)

    def project_pair(i, b):
        pair_copies[i].wait()
        raw = dot(r.shift_s[...], r.wqs[rows_of(b), :], NT).T
        r.raw_s[b] = raw
        cube = raw.reshape(6, hd, toks)
        for c in range(2):
            p0, p1, p2 = cube[3 * c], cube[3 * c + 1], cube[3 * c + 2]
            q = p0 * rms_scale(p0) * gain_s[0]
            k = p1 * rms_scale(p1) * gain_s[1]
            r.qs_send[2 * b + c] = q.astype(BF)
            r.kv_send[2 * b + c] = jnp.concatenate([k, p2], axis=0).astype(BF)

    def start_pair(args, i, b):
        if i < np_ - 1:
            start_to(args, 2 * b)
            start_to(args, 2 * b + 1)
        else:
            start_to(args, sibling)

    project_pair(0, pair_order[0])
    r.tk_send[...] = to_blocks(r.tok[...].astype(F32))
    r.tk_recv[tm] = r.tk_send[tm]
    tk = ("tm", lambda j: r.tk_send.at[j], r.tk_recv, r.tk_sem)
    pl.semaphore_wait(barrier, ns - 1 + nt - 1 + 2)
    start_pair(kv, 0, pair_order[0])
    start_all(*tk)
    for i in range(1, np_):
        project_pair(i, pair_order[i])
        start_pair(kv, i, pair_order[i])
    for i in range(np_):
        start_pair(qs, i, pair_order[i])
    r.kv_recv[sp] = r.kv_send[sp]
    r.qs_recv[sp] = r.qs_send[sp]

    copies["cot"].wait()
    r.cot_send[...] = to_blocks(r.cot[...].astype(F32))
    r.cot_recv[tm] = r.cot_send[tm]
    ct = ("tm", lambda j: r.cot_send.at[j], r.cot_recv, r.cot_sem)
    start_all(*ct)
    copies["val"].wait()
    own_row = r.val[pl.ds(sp, 1), :].astype(F32)
    row_id = lax.broadcasted_iota(jnp.int32, (toks, toks), 0)
    col_id = lax.broadcasted_iota(jnp.int32, (toks, toks), 1)
    own = jnp.broadcast_to(own_row, (toks, toks))
    mask_s = jnp.sum(jnp.where(row_id == col_id, own, 0.0), axis=1, keepdims=True)
    mask_t = jnp.sum(jnp.where(tm * 8 + row_id % 8 == col_id, own, 0.0), axis=1, keepdims=True)


    def unpack(j):
        block = r.kv_recv[j].astype(F32)
        at = pl.ds(pl.multiple_of(j * toks, toks), toks)
        keys, values = block[:hd, :], block[hd:, :]
        bias = jnp.where(r.val[pl.ds(j, 1), :] > 0, 0.0, -1e30)
        r.k_t[:, at] = padded(keys).astype(BF)
        r.v_t[:, at] = padded(values).astype(BF)
        r.k_ref[at, :] = jnp.concatenate([keys, jnp.where(first_row, bias, 0.0)], axis=0).T.astype(BF)
        r.v_ref[at, :] = padded(values).T.astype(BF)

    unpack(sp)
    for b in pair_order[::-1]:
        for j in [sibling] if b is pair_order[-1] else [2 * b, 2 * b + 1]:
            wait_from(*kv, j)
            unpack(j)

    at = ("space", lambda j: r.at_send.at[j], r.at_recv, r.at_sem)

    def two_of(b):
        return pl.ds(pl.multiple_of(b * two, two), two)

    ones = jnp.where(lax.broadcasted_iota(jnp.int32, (hp - hd, two), 0) == 0, 1.0, 0.0)

    def scores_of(i, b):
        for j in [sibling] if i == 0 else [2 * b, 2 * b + 1]:
            wait_from(*qs, j)
        q = jnp.concatenate([r.qs_recv[2 * b + c].astype(F32) for c in range(2)], axis=1)
        r.q_t[:, two_of(b)] = jnp.concatenate([q, ones], axis=0).astype(BF)
        return dot(r.k_ref[...], r.q_t[:, two_of(b)])

    attend_order = [(y + d) % np_ for d in (0, 2, 1, 3)]
    following = scores_of(0, attend_order[0])
    for i, b in enumerate(attend_order):
        scores = following
        top = jnp.max(scores, axis=0, keepdims=True)
        if i < np_ - 1:
            following = scores_of(i + 1, attend_order[i + 1])
        exps = jnp.exp2(scores * power - top * power)
        inverse = 1.0 / jnp.sum(exps, axis=0, keepdims=True)
        exps = exps.astype(BF)
        r.prob[b] = exps
        out = dot(r.v_t[...], exps) * inverse
        r.inverse[b] = inverse
        r.o_ref[b] = out
        for c in range(2):
            r.at_send[2 * b + c] = out[:hd, toks * c : toks * (c + 1)].astype(BF)
        start_pair(at, np_ - 1 if i == 0 else 0, b)
    r.at_recv[sp] = r.at_send[sp]
    wait_all(*at)
    fill = jnp.zeros((z.att_pad - att_w, toks), F32)

    att = jnp.concatenate([r.at_recv[h].astype(F32) for h in range(heads)] + [fill], axis=0).T
    r.aa_send[...] = to_blocks(att)
    r.aa_recv[tm] = r.aa_send[tm]
    aa = ("tm", lambda j: r.aa_send.at[j], r.aa_recv, r.aa_sem)
    start_all(*aa)
    copies["wos"].wait()
    branch = dot(att[:, :att_w].astype(BF), r.wos[...])
    r.mid_o[...] = (r.tok[...].astype(F32) + mask_s * table_s[2:3, :] * branch).astype(BF)

    pair = (dp, tm, sibling)

    def pair_copy(a):
        return remote(
            r.part.at[a, 1 - core], r.pair_recv.at[a], r.pair_sem.at[0, a], r.pair_sem.at[1, a], pair
        )

    def partial_grad(a, att, grad_branch, dims=NN):
        full = dot(att, grad_branch, dims)
        for h in range(heads):
            r.part[a, h % 2, h // 2] = full[hd * h : hd * (h + 1), :].astype(BF)
        pair_copy(a).start()

    def rs_args(kind, a):
        send, recv, sems = (getattr(r, kind + str(a) + end) for end in ("_send", "_recv", "_sem"))
        return (kind, lambda j: send.at[j], recv, sems)

    def total(ref, n):
        value = ref[0].astype(F32)
        for j in range(1, n):
            value = value + ref[j].astype(F32)
        return value

    quarter = width // nx
    rest = quarter - 256

    def rs_y0():
        pair_copy(0).wait_recv()
        for b in range(ny):
            r.y0_send[b] = (r.part[0, core, b].astype(F32) + r.pair_recv[0, b].astype(F32)).astype(BF)
        r.y0_recv[y] = r.y0_send[y]
        start_all(*rs_args("y", 0))

    def rs_x0():
        wait_all(*rs_args("y", 0))
        value = total(r.y0_recv, ny)
        for j in range(nx):
            r.x0_send[j] = value[:, quarter * j : quarter * (j + 1)].astype(BF)
        r.x0_recv[x] = r.x0_send[x]
        start_all(*rs_args("x", 0))

    def rs_x1():
        pair_copy(1).wait_recv()
        value = [r.part[1, core, b].astype(F32) + r.pair_recv[1, b].astype(F32) for b in range(ny)]
        for j in range(nx):
            cols = [v[:, quarter * j : quarter * (j + 1)] for v in value]
            for b in range(ny):
                r.x1_send[j, 2 * b] = cols[b][:, :128].astype(BF)
                r.x1_send[j, 2 * b + 1] = cols[b][:, 128:256].astype(BF)
            r.x1_send[j, 2 * ny] = jnp.concatenate([v[:, 256:] for v in cols], axis=1).astype(BF)
        r.x1_recv[x] = r.x1_send[x]
        start_all(*rs_args("x", 1))

    def rs_y1():
        wait_all(*rs_args("x", 1))
        value = total(r.x1_recv, nx)
        for b in range(ny):
            tail = value[2 * ny][:, rest * b : rest * (b + 1)]
            r.y1_send[b] = jnp.concatenate([value[2 * b], value[2 * b + 1], tail], axis=1).astype(BF)
        r.y1_recv[y] = r.y1_send[y]
        start_all(*rs_args("y", 1))

    third = hd // 3
    own_w = quarter // nz

    def rs_z(a):
        wait_all(*rs_args("x" if a == 0 else "y", a))
        value = total(r.x0_recv, nx) if a == 0 else total(r.y1_recv, ny)
        _, send_of, recv, _ = rs_args("z", a)
        fill = jnp.zeros((third, 128 - 3 * own_w), F32)
        for j in range(nz):
            cols = value[:, own_w * j : own_w * (j + 1)]
            parts = [cols[third * c : third * (c + 1), :] for c in range(3)]
            send_of(j)[...] = jnp.concatenate(parts + [fill], axis=1).astype(BF)
        recv[zz] = send_of(zz)[...]
        start_all(*rs_args("z", a))

    def rs_end(a, out_ref):
        wait_all(*rs_args("z", a))
        value = total(rs_args("z", a)[2], nz)
        cols = [value[:, own_w * c : own_w * (c + 1)] for c in range(3)]
        out_ref[...] = jnp.concatenate(cols, axis=0).T

    def table_args(kind, k):
        send, recv, sems = (getattr(r, k + kind + end) for end in ("_send", "_recv", "_sem"))
        return ({"s": "space", "a": "x"}.get(kind, kind), lambda j: send, recv, sems)

    def table_start(kind, k, value):
        args = table_args(kind, k)
        send = getattr(r, k + kind + "_send")
        send[...] = value.astype(send.dtype)
        args[2][groups[args[0]][1]] = send[...]
        start_all(*args)

    def table_sum(kind, k):
        args = table_args(kind, k)
        wait_all(*args)
        value = args[2][0].astype(F32)
        for j in range(1, groups[args[0]][0]):
            value = value + args[2][j].astype(F32)
        return value

    copies["tab_t"].wait()
    table_t = r.tab_t[...]
    wait_all(*tk)
    wait_all(*ct)
    masked = from_blocks(r.cot_recv[...]) * mask_t
    grad_branch = (masked * table_t[2:3, :]).astype(BF)
    r.gb_t[...] = grad_branch
    copies["wot"].wait()
    r.grad_att[...] = dot(r.wot[...], grad_branch, NT)
    copies["wqt"].wait()
    copies["gn_t"].wait()
    gain_t = gain_columns(r.gn_t)
    for args in (kv, qs, at, tk, ct):
        wait_sent(*args)

    wait_all(*aa)
    att_s = from_blocks(r.aa_recv[...])[:, :att_w].astype(BF)
    r.att_s[...] = att_s
    branch_s = dot(att_s, r.wos[...])
    r.branch_s[...] = branch_s
    middle = from_blocks(r.tk_recv[...]) + mask_t * table_s[2:3, :] * branch_s
    r.mid[...] = middle.astype(BF)
    normed, _ = norm(r.mid[...].astype(F32))
    shifted = (normed * (1.0 + table_t[1:2, :]) + table_t[0:1, :]).astype(BF)
    raw = dot(shifted, r.wqt[...], NT).T.reshape(heads, 3, hd, toks)
    p0, p1, p2 = raw[:, 0], raw[:, 1], raw[:, 2]
    s0, s1 = rms_scale(p0), rms_scale(p1)
    r.p0[...] = p0
    r.p1[...] = p1
    q = p0 * s0 * gain_t[0][None]
    k = p1 * s1 * gain_t[1][None]
    q_f = [padded(q[h]) for h in range(heads)]
    k_f = [padded(k[h]) for h in range(heads)]
    v_f = [padded(p2[h]) for h in range(heads)]
    q_t, k_t, v_t = ([v.astype(BF) for v in part] for part in (q_f, k_f, v_f))
    same = (row_id % 8 == col_id % 8)[None]
    scores = jnp.stack([dot(k_f[h].T.astype(BF), q_t[h]) for h in range(heads)], axis=0)
    scores = jnp.where(same, scores, -1e30)
    exps = jnp.exp2((scores - jnp.max(scores, axis=1, keepdims=True)) * power)
    weights = exps * (1.0 / jnp.sum(exps, axis=1, keepdims=True))
    rounded = weights.astype(BF)
    att = jnp.concatenate([dot(v_t[h], rounded[h])[:hd, :] for h in range(heads)] + [fill], axis=0)
    r.att_f[...] = att
    r.att_t[...] = att[:att_w, :].astype(BF)
    partial_grad(0, r.att_t[...], r.gb_t[...])
    do_t = [padded(r.grad_att[hd * h : hd * (h + 1), :]).astype(BF) for h in range(heads)]
    dw = jnp.stack([dot(v_f[h].T.astype(BF), do_t[h]) for h in range(heads)], axis=0)
    ds = weights * (dw - jnp.sum(dw * weights, axis=1, keepdims=True)) * scaling
    ds = ds.astype(BF)

    def stacked(parts):
        return jnp.stack([v[:hd, :] for v in parts], axis=0).astype(BF).astype(F32)

    dq = stacked([dot(k_t[h], ds[h]) for h in range(heads)])
    dk = stacked([dot(q_t[h], ds[h], NT) for h in range(heads)])
    dv = stacked([dot(do_t[h], rounded[h], NT) for h in range(heads)])
    dq = rms_back(dq * gain_t[0][None], r.p0[...])
    dk = rms_back(dk * gain_t[1][None], r.p1[...])
    grad_raw = jnp.stack([dq, dk, dv], axis=1).reshape(3 * att_w, toks).astype(BF)
    grad_shifted = dot(grad_raw, r.wqt[...], TN)
    normed, inv_t = norm(r.mid[...].astype(F32))
    grad_in, shift_t, scale_t = modulate_back(grad_shifted, normed, inv_t, table_t)
    grad_mid = (from_blocks(r.cot_recv[...]) + grad_in).astype(BF).astype(F32)
    r.grad_mid[...] = grad_mid
    rs_y0()
    grad_branch = (grad_mid * mask_t * table_s[2:3, :]).astype(BF)
    r.gb_s[...] = grad_branch
    grad_att = dot(grad_branch, r.wos[...], NT)
    r.ga_send[...] = to_blocks(
        jnp.concatenate([grad_att, jnp.zeros((toks, z.att_pad - att_w), F32)], axis=1)
    )
    r.ga_recv[tm] = r.ga_send[tm]
    ga = ("tm", lambda j: r.ga_send.at[j], r.ga_recv, r.ga_sem)
    start_all(*ga)

    partial_grad(1, r.att_s[...], r.gb_s[...], TN)
    branch_t = dot(r.att_t[...], r.wot[...], TN)
    gate_t = jnp.sum(from_blocks(r.cot_recv[...]) * mask_t * branch_t, axis=0, keepdims=True)
    gate_s = jnp.sum(r.grad_mid[...] * mask_t * r.branch_s[...], axis=0, keepdims=True)
    r.gm_send[...] = to_blocks(r.grad_mid[...])
    r.gm_recv[tm] = r.gm_send[tm]
    gm = ("tm", lambda j: r.gm_send.at[j], r.gm_recv, r.gm_sem)
    r.ta_send[...] = to_blocks(r.att_f[...].T)
    r.ta_recv[tm] = r.ta_send[tm]
    ta = ("tm", lambda j: r.ta_send.at[j], r.ta_recv, r.ta_sem)
    rs_x1()
    wait_sent(*aa)

    wait_all(*ga)
    grad_att = from_blocks(r.ga_recv[...]).T
    for h in range(heads):
        r.do_send[h] = grad_att[hd * h : hd * (h + 1), :].astype(BF)
    r.do_recv[sp] = r.do_send[sp]
    do = ("space", lambda j: r.do_send.at[j], r.do_recv, r.do_sem, True)
    start_all(*do)
    table_start("s", "e", to_lines([shift_t, scale_t, gate_t, gate_s], z.early))

    lines = width // 128
    ex = ("x", lambda j: r.ex_send.at[j], r.ex_recv, r.ex_sem)

    def early_x():
        value = table_sum("s", "e")
        blank = jnp.zeros((16 - lines, 128), F32)
        for j in range(nx):
            r.ex_send[j] = jnp.concatenate([value[lines * j : lines * (j + 1), :], blank], axis=0)
        r.ex_recv[x] = r.ex_send[x]
        start_all(*ex)

    def early_z():
        wait_all(*ex)
        table_start("z", "e", r.ex_recv[0] + r.ex_recv[1] + r.ex_recv[2] + r.ex_recv[3])

    dqs = ("space", lambda j: r.dq_send.at[j], r.dq_recv, r.dq_sem, True)
    dks = ("space", lambda j: r.dk_send.at[j], r.dk_recv, r.dk_sem, True)
    back_order = [(y + d) % np_ for d in (0, 1, 3, 2)]
    for i, b in enumerate(back_order):
        for j in [sibling] if i == 0 else [2 * b, 2 * b + 1]:
            wait_from(*do, j)
        grad_out = jnp.concatenate([r.do_recv[2 * b + c].astype(F32) for c in range(2)], axis=1)
        grad_out = grad_out * (r.inverse[b] * scaling)
        grad_out = jnp.concatenate([grad_out, jnp.zeros((hp - hd, two), F32)], axis=0).astype(BF)
        shared = jnp.sum(grad_out.astype(F32) * r.o_ref[b], axis=0, keepdims=True)
        exps = r.prob[b]
        ds = (exps.astype(F32) * (dot(r.v_ref[...], grad_out) - shared)).astype(BF)
        dq = dot(r.k_t[...], ds)
        for c in range(2):
            r.dq_send[2 * b + c] = dq[:hd, toks * c : toks * (c + 1)].astype(BF)
        start_pair(dqs, np_ - 1 if i == 0 else 0, b)
        dv = dot(grad_out, exps, NT)
        dk = dot(r.q_t[:, two_of(b)], ds, NT)
        r.dv_t[...] = dv if i == 0 else r.dv_t[...] + dv
        r.dk_t[...] = dk if i == 0 else r.dk_t[...] + dk
        if i == 0:
            start_all(*gm)
        if i == 2:
            rs_x0()
            start_all(*ta)
    for j in range(ns):
        cols = slice(toks * j, toks * (j + 1))
        r.dk_send[j] = jnp.concatenate(
            [r.dk_t[:hd, cols], r.dv_t[:hd, cols] * (1.0 / scaling)], axis=0
        ).astype(BF)
    start_all(*dks)
    r.dq_recv[sp] = r.dq_send[sp]
    r.dk_recv[sp] = r.dk_send[sp]

    rs_y1()
    early_x()
    for args in (ga, do):
        wait_sent(*args)
    pair_copy(0).wait_send()
    pair_copy(1).wait_send()

    normed, inv_s = norm(r.tok[...].astype(F32))
    for i, b in enumerate(back_order):
        for j in [sibling] if i == 0 else [2 * b, 2 * b + 1]:
            wait_from(*dqs, j)
            wait_from(*dks, j)
        raw = r.raw_s[b].reshape(6, hd, toks)
        parts = []
        for c in range(2):
            dq = r.dq_recv[2 * b + c].astype(F32)
            dkv = r.dk_recv[2 * b + c].astype(F32)
            parts.append(rms_back(dq * gain_s[0], raw[3 * c]))
            parts.append(rms_back(dkv[:hd, :] * gain_s[1], raw[3 * c + 1]))
            parts.append(dkv[hd:, :])
        grad_raw = jnp.concatenate(parts, axis=0).astype(BF)
        share = dot(grad_raw, r.wqs[rows_of(b), :], TN)
        r.acc[...] = share if i == 0 else r.acc[...] + share
    grad_in, shift_s, scale_s = modulate_back(r.acc[...], normed, inv_s, table_s)
    table_start("s", "l", to_lines([shift_s, scale_s], z.late))
    rs_z(0)
    table_start("x", "l", table_sum("s", "l"))
    early_z()
    rs_z(1)
    wait_all(*gm)
    r.tgrad[...] = (from_blocks(r.gm_recv[...]) + grad_in).astype(BF)
    results[1].start()
    table_start("z", "l", table_sum("x", "l"))
    wait_all(*ta)
    branch = dot(from_blocks(r.ta_recv[...])[:, :att_w].astype(BF), r.wot[...])
    mixed = r.mid_o[...].astype(F32) + mask_s * table_t[2:3, :] * branch
    r.mixed[...] = mixed.astype(BF)
    results[0].start()
    for args in (dqs, dks, gm, ta, ex):
        wait_sent(*args)
    for a in range(2):
        wait_sent(*rs_args("x", a))
    for a in range(2):
        wait_sent(*rs_args("y", a))
    for args in [table_args("s", "e"), table_args("z", "e"), table_args("s", "l"), table_args("x", "l")]:
        wait_sent(*args)
    wait_sent(*rs_args("z", 0))
    table_start("a", "e", table_sum("z", "e"))
    rs_end(0, r.got)
    results[3].start()
    wait_all(*table_args("a", "e"))
    rs_end(1, r.gos)
    results[2].start()
    wait_sent(*rs_args("z", 1))
    wait_sent(*table_args("a", "e"))
    late = table_sum("z", "l")
    space_rows = [from_lines(late, 0, lines), from_lines(late, 1, lines), from_lines(r.ea_recv[3], 0, lines)]
    for i in range(3):
        r.tabs[i] = jnp.concatenate([space_rows[i], from_lines(r.ea_recv[i], 0, lines)], axis=0)
    results[4].start()
    wait_sent(*table_args("z", "l"))
    for copy in results:
        copy.wait()


def hand_on(*refs):
    n = (len(refs) - 2) // 3
    srcs, dsts, stages, (into, out) = refs[:n], refs[n : 2 * n], refs[2 * n : 3 * n], refs[3 * n :]
    first = [pltpu.make_async_copy(srcs[i], stages[i], into.at[i]) for i in range(n)]
    second = [pltpu.make_async_copy(stages[i], dsts[i], out.at[i]) for i in range(n)]
    for copy in first:
        copy.start()
    for i in range(n):
        first[i].wait()
        second[i].start()
    for copy in second:
        copy.wait()


def solution(mesh):
    nt, ns = mesh.shape["tm"], mesh.shape["space"]

    def on_device(
        tokens, validity, table_space, qkv_space, gains_space, out_space,
        table_time, qkv_time, gains_time, out_time, cotangent,
    ):
        z = Sizes()
        z.width = tokens.shape[3]
        z.toks = tokens.shape[2]
        z.hd = gains_space.shape[1]
        z.heads = out_space.shape[0] // z.hd
        z.ns, z.nt, z.nz = ns, nt, nt // 2
        z.hp = 80
        heads, hd, width, toks, nz, hp = z.heads, z.hd, z.width, z.toks, z.nz, z.hp
        qw, pairs, patches = 3 * heads * hd, ns // 2, ns * toks
        dma = pltpu.SemaphoreType.DMA
        vm = pltpu.VMEM
        z.att_pad = -(-heads * hd // 128) * 128
        z.early, z.late = 40, 32
        scratch = {
            "wqs": vm((qw, width), BF),
            "wos": vm((heads * hd, width), BF),
            "wqt": vm((qw, width), BF),
            "wot": vm((heads * hd, width), BF),
            "tok": vm((toks, width), BF),
            "cot": vm((toks, width), BF),
            "val": vm((ns, toks), jnp.int32),
            "tab_s": vm((3, width), F32),
            "tab_t": vm((3, width), F32),
            "gn_s": vm((2, hd), F32),
            "gn_t": vm((2, hd), F32),
            "q_sem": dma((pairs,)),
            "w_sem": dma((10,)),
            "shift_s": vm((toks, width), BF),
            "raw_s": vm((pairs, 6 * hd, toks), F32),
            "p0": vm((heads, hd, toks), F32),
            "p1": vm((heads, hd, toks), F32),
            "q_t": vm((hp, patches), BF),
            "k_t": vm((hp, patches), BF),
            "v_t": vm((hp, patches), BF),
            "k_ref": vm((patches, hp), BF),
            "v_ref": vm((patches, hp), BF),
            "prob": vm((pairs, patches, 2 * toks), BF),
            "inverse": vm((pairs, 1, 2 * toks), F32),
            "o_ref": vm((pairs, hp, 2 * toks), F32),
            "dk_t": vm((hp, patches), F32),
            "dv_t": vm((hp, patches), F32),
            "att_s": vm((toks, heads * hd), BF),
            "mid": vm((toks, width), BF),
            "mid_o": vm((toks, width), BF),
            "att_f": vm((z.att_pad, toks), F32),
            "att_t": vm((heads * hd, toks), BF),
            "branch_s": vm((toks, width), F32),
            "grad_att": vm((heads * hd, toks), F32),
            "grad_mid": vm((toks, width), F32),
            "acc": vm((toks, width), F32),
            "gb_t": vm((toks, width), BF),
            "gb_s": vm((toks, width), BF),
            "part": vm((2, 2, pairs, hd, width), BF),
            "pair_recv": vm((2, pairs, hd, width), BF),
            "pair_sem": dma((2, 2)),
        }

        def both(name, n, shape, dtype, arrivals=1):
            scratch[name + "_send"] = vm((n,) + shape, dtype)
            scratch[name + "_recv"] = vm((n,) + shape, dtype)
            scratch[name + "_sem"] = dma((1 + arrivals,))

        both("kv", ns, (2 * hd, toks), BF, ns)
        both("qs", ns, (hd, toks), BF, ns)
        both("dq", ns, (hd, toks), BF, ns)
        both("dk", ns, (2 * hd, toks), BF, ns)
        both("at", ns, (hd, toks), BF)
        both("do", ns, (hd, toks), BF, ns)
        for name in ("tk", "cot", "gm"):
            both(name, nt, (width // 16, 128), BF)
        for name in ("aa", "ga", "ta"):
            both(name, nt, (z.att_pad // 16, 128), BF)
        both("y0", pairs, (hd, width), BF)
        both("x0", 4, (hd, width // 4), BF)
        both("x1", 4, (2 * pairs + 1, hd, 128), BF)
        both("y1", pairs, (hd, width // 4), BF)
        both("z0", nz, (hd // 3, 128), BF)
        both("z1", nz, (hd // 3, 128), BF)

        def rows(name, n, lines, dtype=F32):
            scratch[name + "_send"] = vm((lines, 128), dtype)
            scratch[name + "_recv"] = vm((n, lines, 128), dtype)
            scratch[name + "_sem"] = dma((2,))

        both("ex", 4, (16, 128), F32)
        rows("es", ns, z.early)
        rows("ez", nz, 16, BF)
        rows("ea", 4, 16)
        rows("ls", ns, z.late)
        rows("lx", 4, z.late)
        rows("lz", nz, z.late, BF)

        ins = [v + "_in" for v in ("tok", "cot", "val", "tab_s", "gn_s", "tab_t", "gn_t")]
        ins += ["qkv_s", "out_s", "qkv_t", "out_t"]
        names = ["mixed", "tgrad", "gos", "got", "tabs"]
        outs = [v + "_out" for v in names]
        shapes = [
            jax.ShapeDtypeStruct((toks, width), BF),
            jax.ShapeDtypeStruct((toks, width), BF),
            jax.ShapeDtypeStruct((width // 4 // nz, hd), F32),
            jax.ShapeDtypeStruct((width // 4 // nz, hd), F32),
            jax.ShapeDtypeStruct((3, 2, width), F32),
        ]
        for name, shape in zip(names, shapes):
            scratch[name] = vm(shape.shape, shape.dtype)
        scratch["o_sem"] = dma((5,))
        vmem = pl.BlockSpec(memory_space=pltpu.VMEM)
        anywhere = pl.BlockSpec(memory_space=pl.ANY)
        results = pl.pallas_call(
            functools.partial(kernel, z, ins + outs + list(scratch)),
            out_shape=shapes,
            in_specs=[anywhere] * 11,
            out_specs=[anywhere] * 5,
            scratch_shapes=list(scratch.values()),
            compiler_params=pltpu.CompilerParams(
                collective_id=0, has_side_effects=True, vmem_limit_bytes=62 * 1024 * 1024
            ),
        )(
            tokens.reshape(toks, width),
            cotangent.reshape(toks, width),
            validity.reshape(ns, toks),
            table_space,
            gains_space,
            table_time,
            gains_time,
            qkv_space.T,
            out_space,
            qkv_time.T,
            out_time,
        )
        mixed, tgrad, gos, got, tabs = pl.pallas_call(
            hand_on,
            out_shape=[jax.ShapeDtypeStruct(v.shape, v.dtype) for v in results],
            in_specs=[anywhere] * 5,
            out_specs=[anywhere] * 5,
            scratch_shapes=[vm(v.shape, v.dtype) for v in results] + [dma((5,)), dma((5,))],
        )(*results)
        shape = tokens.shape
        return mixed.reshape(shape), tgrad.reshape(shape), gos.T, got.T, tabs.transpose(1, 0, 2)

    spread = P("dp", "tm", "space", None)
    return jax.shard_map(
        on_device,
        mesh=mesh,
        in_specs=(spread,) + (P(),) * 9 + (spread,),
        out_specs=(spread, spread, P("space", ("dp", "tm")), P("space", ("dp", "tm")), P()),
        check_vma=False,
    )
```

time: 95.6 us -> 72.8 us (0.76); the launches traced: 94.3 us -> 72.7 us
  Pallas kernels: 93.6 us -> 71.9 us
    pallas_call x1, Pallas kernels: 91.7 us -> 70 us  [on_device(): pl.pallas_call(functools.partial(kernel, z, ins + outs + list(scratch)),...]
where the time goes in v2:
time: 72.8 us; the launch traced here: 72.7 us
  Pallas kernels  71.9 us (99%)
  between operations  0.8 us (1%)
    pallas_call x1, Pallas kernels, on_device(): pl.pallas_call(functools.partial(kernel, z, ins + outs + list(scratch)),...  70 us
    pallas_call x1, Pallas kernels, on_device(): pl.pallas_call(hand_on, out_shape=[jax.ShapeDtypeStruct(v.shape, v.dtype)...  1.87 us

profile of v2, /device:TPU:32, one launch (start us, length us, event | category | flops | bytes accessed | tf_op | source)
XLA Modules:
  0.0 72.7 jit_solution(4725610791900478311)
XLA Ops:
  0.6 70.0 %shard_map.146 = (bf16[128,1152]{1,0:T(8,128)(2,1)}, bf16[128,1152]{1,0:T(8,128)(2,1)}, f32[36,72]{1,0:T(8,128)}, f32[36,72]{1,0:T(8,128)}, f32[3,2,1152]{2,1,0:T(2,128)}) custom-call(bf16[128,1152]{1,0:T(8,128)(2,1)} %bitcast.12, bf16[128,1152]{1,0:T(8,128)(2,1)} %bitcast.13, s32[8,128]{1,0:T(8,128)} %bitcast.14, f32[3,1152]{1,0:T(4,128)} %refs_3_.1, ...), custom_call_target="tpu_custom_call" | custom-call | tf_op jit(solution)/shard_map/pallas_call | solution.py:795
  70.6 1.9 %shard_map.147 = (bf16[128,1152]{1,0:T(8,128)(2,1)}, bf16[128,1152]{1,0:T(8,128)(2,1)}, f32[36,72]{1,0:T(8,128)}, f32[36,72]{1,0:T(8,128)}, f32[3,2,1152]{2,1,0:T(2,128)}) custom-call(bf16[128,1152]{1,0:T(8,128)(2,1)} %get-tuple-element.15.refs_0_, bf16[128,1152]{1,0:T(8,128)(2,1)} %get-tuple-element.16.refs_1_, f32[36,72]{1,0:T(8,128)} %get-tuple-element.17.refs_2_, ...), custom_call_target="tpu_custom_call" | custom-call | tf_op jit(solution)/shard_map/pallas_call | solution.py:817

commit v3 on v2

--- a/solution.py
+++ b/solution.py
@@ -161,12 +161,10 @@
 
     def greet(group):
         n, me, device = groups[group]
-
-        def body(d, carry):
+        for d in order[group]:
             signal(device((me + d) % n))
-            return carry
-
-        lax.fori_loop(1, n, body, 0)
+
+    greet("space")
 
     pair_order = [(y + d) % np_ for d in (2, 1, 3, 0)]
 
@@ -209,7 +207,6 @@
     for name in ("tok", "tab_s", "gn_s"):
         copies[name].start()
     pair_copies[0].start()
-    greet("space")
     greet("tm")
     other = 1 - dp
     signal((other, tm, sp))
@@ -455,8 +452,10 @@
     copies["tab_t"].wait()
     table_t = r.tab_t[...]
     wait_all(*tk)
+    r.tok_t[...] = from_blocks(r.tk_recv[...])
     wait_all(*ct)
-    masked = from_blocks(r.cot_recv[...]) * mask_t
+    r.cot_t[...] = from_blocks(r.cot_recv[...])
+    masked = r.cot_t[...] * mask_t
     grad_branch = (masked * table_t[2:3, :]).astype(BF)
     r.gb_t[...] = grad_branch
     copies["wot"].wait()
@@ -472,9 +471,10 @@
     r.att_s[...] = att_s
     branch_s = dot(att_s, r.wos[...])
     r.branch_s[...] = branch_s
-    middle = from_blocks(r.tk_recv[...]) + mask_t * table_s[2:3, :] * branch_s
+    middle = r.tok_t[...] + mask_t * table_s[2:3, :] * branch_s
     r.mid[...] = middle.astype(BF)
-    normed, _ = norm(r.mid[...].astype(F32))
+    normed, inv_t = norm(r.mid[...].astype(F32))
+    r.acc[...] = normed
     shifted = (normed * (1.0 + table_t[1:2, :]) + table_t[0:1, :]).astype(BF)
     raw = dot(shifted, r.wqt[...], NT).T.reshape(heads, 3, hd, toks)
     p0, p1, p2 = raw[:, 0], raw[:, 1], raw[:, 2]
@@ -512,9 +512,8 @@
     dk = rms_back(dk * gain_t[1][None], r.p1[...])
     grad_raw = jnp.stack([dq, dk, dv], axis=1).reshape(3 * att_w, toks).astype(BF)
     grad_shifted = dot(grad_raw, r.wqt[...], TN)
-    normed, inv_t = norm(r.mid[...].astype(F32))
-    grad_in, shift_t, scale_t = modulate_back(grad_shifted, normed, inv_t, table_t)
-    grad_mid = (from_blocks(r.cot_recv[...]) + grad_in).astype(BF).astype(F32)
+    grad_in, shift_t, scale_t = modulate_back(grad_shifted, r.acc[...], inv_t, table_t)
+    grad_mid = (r.cot_t[...] + grad_in).astype(BF).astype(F32)
     r.grad_mid[...] = grad_mid
     rs_y0()
     grad_branch = (grad_mid * mask_t * table_s[2:3, :]).astype(BF)
@@ -529,7 +528,7 @@
 
     partial_grad(1, r.att_s[...], r.gb_s[...], TN)
     branch_t = dot(r.att_t[...], r.wot[...], TN)
-    gate_t = jnp.sum(from_blocks(r.cot_recv[...]) * mask_t * branch_t, axis=0, keepdims=True)
+    gate_t = jnp.sum(r.cot_t[...] * mask_t * branch_t, axis=0, keepdims=True)
     gate_s = jnp.sum(r.grad_mid[...] * mask_t * r.branch_s[...], axis=0, keepdims=True)
     r.gm_send[...] = to_blocks(r.grad_mid[...])
     r.gm_recv[tm] = r.gm_send[tm]
@@ -547,7 +546,7 @@
     r.do_recv[sp] = r.do_send[sp]
     do = ("space", lambda j: r.do_send.at[j], r.do_recv, r.do_sem, True)
     start_all(*do)
-    table_start("s", "e", to_lines([shift_t, scale_t, gate_t, gate_s], z.early))
+    early_rows = to_lines([shift_t, scale_t, gate_t, gate_s], z.early)
 
     lines = width // 128
     ex = ("x", lambda j: r.ex_send.at[j], r.ex_recv, r.ex_sem)
@@ -586,6 +585,8 @@
         r.dk_t[...] = dk if i == 0 else r.dk_t[...] + dk
         if i == 0:
             start_all(*gm)
+        if i == 1:
+            table_start("s", "e", early_rows)
         if i == 2:
             rs_x0()
             start_all(*ta)
@@ -599,7 +600,6 @@
     r.dk_recv[sp] = r.dk_send[sp]
 
     rs_y1()
-    early_x()
     for args in (ga, do):
         wait_sent(*args)
     pair_copy(0).wait_send()
@@ -621,6 +621,8 @@
         grad_raw = jnp.concatenate(parts, axis=0).astype(BF)
         share = dot(grad_raw, r.wqs[rows_of(b), :], TN)
         r.acc[...] = share if i == 0 else r.acc[...] + share
+        if i == 0:
+            early_x()
     grad_in, shift_s, scale_s = modulate_back(r.acc[...], normed, inv_s, table_s)
     table_start("s", "l", to_lines([shift_s, scale_s], z.late))
     rs_z(0)
@@ -696,7 +698,7 @@
         dma = pltpu.SemaphoreType.DMA
         vm = pltpu.VMEM
         z.att_pad = -(-heads * hd // 128) * 128
-        z.early, z.late = 40, 32
+        z.early, z.late = 48, 32
         scratch = {
             "wqs": vm((qw, width), BF),
             "wos": vm((heads * hd, width), BF),
@@ -731,6 +733,8 @@
             "att_f": vm((z.att_pad, toks), F32),
             "att_t": vm((heads * hd, toks), BF),
             "branch_s": vm((toks, width), F32),
+            "tok_t": vm((toks, width), F32),
+            "cot_t": vm((toks, width), F32),
             "grad_att": vm((heads * hd, toks), F32),
             "grad_mid": vm((toks, width), F32),
             "acc": vm((toks, width), F32),
@@ -769,7 +773,7 @@
             scratch[name + "_sem"] = dma((2,))
 
         both("ex", 4, (16, 128), F32)
-        rows("es", ns, z.early)
+        rows("es", ns, z.early, BF)
         rows("ez", nz, 16, BF)
         rows("ea", 4, 16)
         rows("ls", ns, z.late)

time: 72.8 us -> 72.6 us (level); the launches traced: 72.7 us -> 71.7 us
  Pallas kernels: 71.9 us -> 70.9 us
    pallas_call x1, Pallas kernels: 70 us -> 69 us  [on_device(): pl.pallas_call(functools.partial(kernel, z, ins + outs + list(scratch)),...]
where the time goes in v3:
time: 72.6 us; the launch traced here: 71.7 us
  Pallas kernels  70.9 us (98%)
  between operations  0.8 us (1%)
    pallas_call x1, Pallas kernels, on_device(): pl.pallas_call(functools.partial(kernel, z, ins + outs + list(scratch)),...  69 us
    pallas_call x1, Pallas kernels, on_device(): pl.pallas_call(hand_on, out_shape=[jax.ShapeDtypeStruct(v.shape, v.dtype)...  1.87 us

profile of v3, /device:TPU:32, one launch (start us, length us, event | category | flops | bytes accessed | tf_op | source)
XLA Modules:
  0.0 71.7 jit_solution(9673605175844794104)
XLA Ops:
  0.6 69.0 %shard_map.146 = (bf16[128,1152]{1,0:T(8,128)(2,1)}, bf16[128,1152]{1,0:T(8,128)(2,1)}, f32[36,72]{1,0:T(8,128)}, f32[36,72]{1,0:T(8,128)}, f32[3,2,1152]{2,1,0:T(2,128)}) custom-call(bf16[128,1152]{1,0:T(8,128)(2,1)} %bitcast.12, bf16[128,1152]{1,0:T(8,128)(2,1)} %bitcast.13, s32[8,128]{1,0:T(8,128)} %bitcast.14, f32[3,1152]{1,0:T(4,128)} %refs_3_.1, ...), custom_call_target="tpu_custom_call" | custom-call | tf_op jit(solution)/shard_map/pallas_call | solution.py:799
  69.6 1.9 %shard_map.147 = (bf16[128,1152]{1,0:T(8,128)(2,1)}, bf16[128,1152]{1,0:T(8,128)(2,1)}, f32[36,72]{1,0:T(8,128)}, f32[36,72]{1,0:T(8,128)}, f32[3,2,1152]{2,1,0:T(2,128)}) custom-call(bf16[128,1152]{1,0:T(8,128)(2,1)} %get-tuple-element.15.refs_0_, bf16[128,1152]{1,0:T(8,128)(2,1)} %get-tuple-element.16.refs_1_, f32[36,72]{1,0:T(8,128)} %get-tuple-element.17.refs_2_, ...), custom_call_target="tpu_custom_call" | custom-call | tf_op jit(solution)/shard_map/pallas_call | solution.py:821
